TPU v7x, 256 devices: a whole 4x4x8 slice. The times are simulated.
256 devices in a mesh: row: 16 (over y_lo, x, core), col: 16 (over y_hi, z).
Axes of the slice: x: 4, y: 4 (y_hi: 2, y_lo: 2; y = y_hi * 2 + y_lo), z: 8, core: 2. Of those that a mesh axis runs over, the one named last changes fastest.
Arguments:
- frame_first: float32 [4, 4096, 4096], P(None, 'row', 'col'), may hold values from -10 to 10
- frame_second: float32 [4, 4096, 4096], P(None, 'row', 'col'), may hold values from -10 to 10
- shifts: int32 [16, 16, 2], P('row', 'col'), may hold values from -4 to 4, as said below
Outputs:
- flow_field: float32 [2, 4096, 4096], P(None, 'row', 'col')
- coarse_flow: float32 [2, 512, 512], P(None, 'row', 'col')
Inputs may be any that keep to these rules, and one draw needn't show every extreme that they name: `shifts`: some tile has displacement 4 along rows and some tile -4 along columns.
All inputs are finite; a program needn't handle non-finite values.
Results may differ from a plain program's by a relative error of at most 0.0003.
Values sent between devices are 32-bit elements; how exact they have to be, the bound alone decides.
A program may use at most 64 MiB of HBM per device.

v0:
```python
import jax
import jax.numpy as jnp
from jax import lax
from jax.sharding import PartitionSpec as P

FACTOR = 8
MAXD = 4
ITERS_C = 3
ITERS_F = 3


tau_step = 0.25
sigma_step = 0.25
data_weight = 0.3
smooth_weight = 0.3


def extended_2(cells, sides, width):
    for axis, dim in sides:
        count = lax.axis_size(axis)
        ends = count - 1
        head = lax.slice_in_dim(cells, 0, width, axis=dim)
        tail = lax.slice_in_dim(cells, cells.shape[dim] - width, cells.shape[dim], axis=dim)
        cells = jnp.concatenate(
            [
                lax.ppermute(tail, axis, [(i, (i + 1) % count) for i in range(ends)]),
                cells,
                lax.ppermute(head, axis, [((i + 1) % count, i) for i in range(ends)]),
            ],
            axis=dim,
        )
    return cells


def pad_rows(field_in):
    return extended_2(field_in, (("row", 1),), 1)


def pad_cols(field_in):
    return extended_2(field_in, (("col", 2),), 1)


def central_rows(padded):
    return 0.5 * (padded[:, 2:, :] - padded[:, :-2, :])


def central_cols(padded):
    return 0.5 * (padded[:, :, 2:] - padded[:, :, :-2])


def primal_dual(initial, grad_rows, grad_cols, offset, iterations, zero_start):
    flow_now = initial
    extrapolated = initial
    dual_rows = jnp.zeros_like(initial)
    dual_cols = jnp.zeros_like(initial)
    dual_data = jnp.zeros_like(offset)
    for iteration in range(iterations):
        if not (zero_start and iteration == 0):
            dual_rows = dual_rows + sigma_step * central_rows(pad_rows(extrapolated))
            dual_cols = dual_cols + sigma_step * central_cols(pad_cols(extrapolated))
        shrink_factor = jnp.maximum(
            1.0, jnp.sqrt(dual_rows * dual_rows + dual_cols * dual_cols) / smooth_weight
        )
        dual_rows = dual_rows / shrink_factor
        dual_cols = dual_cols / shrink_factor
        residual = offset + grad_rows * extrapolated[0:1] + grad_cols * extrapolated[1:2]
        dual_data = jnp.clip(dual_data + sigma_step * residual, -data_weight, data_weight)
        divergence = central_rows(pad_rows(dual_rows)) + central_cols(pad_cols(dual_cols))
        data_pull = jnp.stack(
            [jnp.sum(dual_data * grad_rows, axis=0), jnp.sum(dual_data * grad_cols, axis=0)]
        )
        flow_next = flow_now + tau_step * (divergence - data_pull)
        extrapolated = 2.0 * flow_next - flow_now
        flow_now = flow_next
    return flow_now


def local(frame_first, frame_second, shifts):
    band_count, tile_height, tile_width = frame_first.shape
    coarse_height = tile_height // FACTOR
    coarse_width = tile_width // FACTOR
    coarse_first = frame_first.reshape(
        band_count, coarse_height, FACTOR, coarse_width, FACTOR
    ).mean(axis=(2, 4))
    coarse_second = frame_second.reshape(
        band_count, coarse_height, FACTOR, coarse_width, FACTOR
    ).mean(axis=(2, 4))
    tile_rows = central_rows(pad_rows(coarse_second))
    tile_cols = central_cols(pad_cols(coarse_second))
    tile_zero = jnp.zeros((2, coarse_height, coarse_width), jnp.float32)
    coarse_result = primal_dual(
        tile_zero, tile_rows, tile_cols, coarse_second - coarse_first, ITERS_C, True
    )
    initial = FACTOR * jnp.repeat(jnp.repeat(coarse_result, FACTOR, axis=1), FACTOR, axis=2)
    offsets = shifts[0, 0]
    extended = extended_2(frame_second, (("row", 1), ("col", 2)), MAXD + 1)
    corner = (jnp.int32(0), MAXD + offsets[0], MAXD + offsets[1])
    window = lax.dynamic_slice(extended, corner, (band_count, tile_height + 2, tile_width + 2))
    warped = window[:, 1:-1, 1:-1]
    grad_rows = 0.5 * (window[:, 2:, 1:-1] - window[:, :-2, 1:-1])
    grad_cols = 0.5 * (window[:, 1:-1, 2:] - window[:, 1:-1, :-2])
    offset = warped - frame_first - grad_rows * initial[0:1] - grad_cols * initial[1:2]
    flow_result = primal_dual(initial, grad_rows, grad_cols, offset, ITERS_F, False)
    return (flow_result, coarse_result)


def solution(mesh):
    return jax.shard_map(
        local,
        mesh=mesh,
        in_specs=(P(None, "row", "col"), P(None, "row", "col"), P("row", "col", None)),
        out_specs=(P(None, "row", "col"), P(None, "row", "col")),
        check_vma=False,
    )
```

profile of v0, /device:TPU:24, one launch (start us, length us, event | category | flops | bytes accessed | tf_op | source)
XLA Modules:
  0.0 325.4 jit_solution(13923199146931667450)
XLA Ops:
  0.6 12.2 %reshape.72 = f32[4,32,8,32,8]{4,3,2,1,0:T(8,128)} reshape(f32[4,256,256]{2,1,0:T(8,128)} %param.4) | data formatting | bytes 2097152 | tf_op jit(solution)/shard_map/reshape | solution.py:85
  12.8 7.1 %reduce_sum.126 = f32[4,32,32]{2,1,0:T(8,128)S(1)} reduce(f32[4,32,8,32,8]{4,3,2,1,0:T(8,128)} %reshape.72, f32[]{:T(128)} %constant.52.clone.1), dimensions={2,4}, to_apply=%region_0.0 | reduce | flops 258048 | bytes 1064964 | tf_op jit(solution)/shard_map/reduce_sum | solution.py:87
  21.9 5.8 %collective-permute-start.4 = (f32[4,1,32]{2,1,0:T(1,128)S(1)}, f32[4,1,32]{2,1,0:T(1,128)S(1)}, u32[]{:S(2)}, u32[]{:S(2)}) collective-permute-start(f32[4,1,32]{2,1,0:T(1,128)S(1)} %get-tuple-element.77), channel_id=1, source_target_pairs={{16,0},{32,16},{48,32},{64,48},{80,64},{96,80},{112,96},{128,112},... | collective-permute-start | bytes 1544 | tf_op jit(solution)/shard_map/ppermute | solution.py:28
  31.5 6.5 %collective-permute-start.6 = (f32[4,32,1]{2,1,0:T(8,128)S(1)}, f32[4,32,1]{2,1,0:T(8,128)S(1)}, u32[]{:S(2)}, u32[]{:S(2)}) collective-permute-start(f32[4,32,1]{2,1,0:T(8,128)S(1)} %get-tuple-element.75), channel_id=1, source_target_pairs={{1,0},{2,1},{3,2},{4,3},{5,4},{6,5},{7,6},{8,7},{9,8},{10,9},{11,1... | collective-permute-start | bytes 1544 | tf_op jit(solution)/shard_map/ppermute | solution.py:28
  40.0 11.3 %reshape.73 = f32[4,32,8,32,8]{4,3,2,1,0:T(8,128)} reshape(f32[4,256,256]{2,1,0:T(8,128)S(1)} %copy-done.12) | data formatting | bytes 2097152 | tf_op jit(solution)/shard_map/reshape | solution.py:82
  56.2 7.0 %reduce_sum.127 = f32[4,32,32]{2,1,0:T(8,128)S(1)} reduce(f32[4,32,8,32,8]{4,3,2,1,0:T(8,128)} %reshape.73, f32[]{:T(128)} %constant.52.clone.1), dimensions={2,4}, to_apply=%region_1.0 | reduce | flops 258048 | bytes 1064964 | tf_op jit(solution)/shard_map/reduce_sum | solution.py:84
  65.3 7.5 %collective-permute-start.2 = (f32[2,32,1]{2,1,0:T(8,128)S(1)}, f32[2,32,1]{2,1,0:T(8,128)S(1)}, u32[]{:S(2)}, u32[]{:S(2)}) collective-permute-start(f32[2,32,1]{2,1,0:T(8,128)S(1)} %broadcast.150), channel_id=1, source_target_pairs={{1,0},{2,1},{3,2},{4,3},{5,4},{6,5},{7,6},{8,7},{9,8},{10,9},{11,1... | collective-permute-start | bytes 776 | tf_op jit(solution)/shard_map/ppermute | solution.py:28
  74.8 5.8 %collective-permute-start = (f32[2,1,32]{2,1,0:T(1,128)S(1)}, f32[2,1,32]{2,1,0:T(1,128)S(1)}, u32[]{:S(2)}, u32[]{:S(2)}) collective-permute-start(f32[2,1,32]{2,1,0:T(1,128)S(1)} %broadcast.149), channel_id=1, source_target_pairs={{16,0},{32,16},{48,32},{64,48},{80,64},{96,80},{112,96},{128,112},... | collective-permute-start | bytes 776 | tf_op jit(solution)/shard_map/ppermute | solution.py:28
  92.4 7.5 %collective-permute-start.10 = (f32[2,32,1]{2,1,0:T(8,128)S(1)}, f32[2,32,1]{2,1,0:T(8,128)S(1)}, u32[]{:S(2)}, u32[]{:S(2)}) collective-permute-start(f32[2,32,1]{2,1,0:T(8,128)S(1)} %get-tuple-element.95), channel_id=1, source_target_pairs={{1,0},{2,1},{3,2},{4,3},{5,4},{6,5},{7,6},{8,7},{9,8},{10,9},{11,1... | collective-permute-start | bytes 776 | tf_op jit(solution)/shard_map/ppermute | solution.py:28
  103.7 7.8 %collective-permute-start.14 = (f32[2,32,1]{2,1,0:T(8,128)S(1)}, f32[2,32,1]{2,1,0:T(8,128)S(1)}, u32[]{:S(2)}, u32[]{:S(2)}) collective-permute-start(f32[2,32,1]{2,1,0:T(8,128)S(1)} %get-tuple-element.93), channel_id=1, source_target_pairs={{1,0},{2,1},{3,2},{4,3},{5,4},{6,5},{7,6},{8,7},{9,8},{10,9},{11,1... | collective-permute-start | bytes 776 | tf_op jit(solution)/shard_map/ppermute | solution.py:28
  113.5 5.8 %collective-permute-start.12 = (f32[2,1,32]{2,1,0:T(1,128)S(1)}, f32[2,1,32]{2,1,0:T(1,128)S(1)}, u32[]{:S(2)}, u32[]{:S(2)}) collective-permute-start(f32[2,1,32]{2,1,0:T(1,128)S(1)} %get-tuple-element.91), channel_id=1, source_target_pairs={{16,0},{32,16},{48,32},{64,48},{80,64},{96,80},{112,96},{128,112},... | collective-permute-start | bytes 776 | tf_op jit(solution)/shard_map/ppermute | solution.py:28
  122.6 5.8 %collective-permute-start.16 = (f32[2,1,32]{2,1,0:T(1,128)S(1)}, f32[2,1,32]{2,1,0:T(1,128)S(1)}, u32[]{:S(2)}, u32[]{:S(2)}) collective-permute-start(f32[2,1,32]{2,1,0:T(1,128)S(1)} %get-tuple-element.87), channel_id=1, source_target_pairs={{16,0},{32,16},{48,32},{64,48},{80,64},{96,80},{112,96},{128,112},... | collective-permute-start | bytes 776 | tf_op jit(solution)/shard_map/ppermute | solution.py:28
  130.3 7.5 %collective-permute-start.18 = (f32[2,32,1]{2,1,0:T(8,128)S(1)}, f32[2,32,1]{2,1,0:T(8,128)S(1)}, u32[]{:S(2)}, u32[]{:S(2)}) collective-permute-start(f32[2,32,1]{2,1,0:T(8,128)S(1)} %get-tuple-element.85), channel_id=1, source_target_pairs={{1,0},{2,1},{3,2},{4,3},{5,4},{6,5},{7,6},{8,7},{9,8},{10,9},{11,1... | collective-permute-start | bytes 776 | tf_op jit(solution)/shard_map/ppermute | solution.py:28
  141.6 7.8 %collective-permute-start.22 = (f32[2,32,1]{2,1,0:T(8,128)S(1)}, f32[2,32,1]{2,1,0:T(8,128)S(1)}, u32[]{:S(2)}, u32[]{:S(2)}) collective-permute-start(f32[2,32,1]{2,1,0:T(8,128)S(1)} %get-tuple-element.83), channel_id=1, source_target_pairs={{1,0},{2,1},{3,2},{4,3},{5,4},{6,5},{7,6},{8,7},{9,8},{10,9},{11,1... | collective-permute-start | bytes 776 | tf_op jit(solution)/shard_map/ppermute | solution.py:28
  151.4 5.8 %collective-permute-start.20 = (f32[2,1,32]{2,1,0:T(1,128)S(1)}, f32[2,1,32]{2,1,0:T(1,128)S(1)}, u32[]{:S(2)}, u32[]{:S(2)}) collective-permute-start(f32[2,1,32]{2,1,0:T(1,128)S(1)} %get-tuple-element.81), channel_id=1, source_target_pairs={{16,0},{32,16},{48,32},{64,48},{80,64},{96,80},{112,96},{128,112},... | collective-permute-start | bytes 776 | tf_op jit(solution)/shard_map/ppermute | solution.py:28
  162.5 5.8 %collective-permute-start.24 = (f32[2,1,256]{2,1,0:T(1,128)S(1)}, f32[2,1,256]{2,1,0:T(1,128)S(1)}, u32[]{:S(2)}, u32[]{:S(2)}) collective-permute-start(f32[2,1,256]{2,1,0:T(1,128)S(1)} %get-tuple-element.71), channel_id=1, source_target_pairs={{16,0},{32,16},{48,32},{64,48},{80,64},{96,80},{112,96},{128,112},... | collective-permute-start | bytes 6152 | tf_op jit(solution)/shard_map/ppermute | solution.py:28
  170.2 7.5 %collective-permute-start.26 = (f32[2,256,1]{2,1,0:T(8,128)S(1)}, f32[2,256,1]{2,1,0:T(8,128)S(1)}, u32[]{:S(2)}, u32[]{:S(2)}) collective-permute-start(f32[2,256,1]{2,1,0:T(8,128)S(1)} %get-tuple-element.69), channel_id=1, source_target_pairs={{1,0},{2,1},{3,2},{4,3},{5,4},{6,5},{7,6},{8,7},{9,8},{10,9},{11,1... | collective-permute-start | bytes 6152 | tf_op jit(solution)/shard_map/ppermute | solution.py:28
  185.1 8.0 %collective-permute-start.30 = (f32[2,256,1]{2,1,0:T(8,128)}, f32[2,256,1]{2,1,0:T(8,128)}, u32[]{:S(2)}, u32[]{:S(2)}) collective-permute-start(f32[2,256,1]{2,1,0:T(8,128)} %get-tuple-element.67), channel_id=1, source_target_pairs={{1,0},{2,1},{3,2},{4,3},{5,4},{6,5},{7,6},{8,7},{9,8},{10,9},{11,1... | collective-permute-start | bytes 6152 | tf_op jit(solution)/shard_map/ppermute | solution.py:28
  195.2 7.5 %collective-permute-start.35 = (f32[4,266,5]{1,2,0:T(8,128)S(1)}, f32[4,266,5]{1,2,0:T(8,128)S(1)}, u32[]{:S(2)}, u32[]{:S(2)}) collective-permute-start(f32[4,266,5]{1,2,0:T(8,128)S(1)} %get-tuple-element.39), channel_id=1, source_target_pairs={{1,0},{2,1},{3,2},{4,3},{5,4},{6,5},{7,6},{8,7},{9,8},{10,9},{11,1... | collective-permute-start | bytes 63848 | tf_op jit(solution)/shard_map/ppermute | solution.py:28
  204.7 6.1 %collective-permute-start.28 = (f32[2,1,256]{2,1,0:T(1,128)S(1)}, f32[2,1,256]{2,1,0:T(1,128)S(1)}, u32[]{:S(2)}, u32[]{:S(2)}) collective-permute-start(f32[2,1,256]{2,1,0:T(1,128)S(1)} %get-tuple-element.65), channel_id=1, source_target_pairs={{16,0},{32,16},{48,32},{64,48},{80,64},{96,80},{112,96},{128,112},... | collective-permute-start | bytes 6152 | tf_op jit(solution)/shard_map/ppermute | solution.py:28
  231.9 7.5 %collective-permute-start.38 = (f32[2,256,1]{2,1,0:T(8,128)}, f32[2,256,1]{2,1,0:T(8,128)}, u32[]{:S(2)}, u32[]{:S(2)}) collective-permute-start(f32[2,256,1]{2,1,0:T(8,128)} %get-tuple-element.59), channel_id=1, source_target_pairs={{1,0},{2,1},{3,2},{4,3},{5,4},{6,5},{7,6},{8,7},{9,8},{10,9},{11,1... | collective-permute-start | bytes 6152 | tf_op jit(solution)/shard_map/ppermute | solution.py:28
  250.2 7.7 %collective-permute-start.42 = (f32[2,256,1]{2,1,0:T(8,128)}, f32[2,256,1]{2,1,0:T(8,128)}, u32[]{:S(2)}, u32[]{:S(2)}) collective-permute-start(f32[2,256,1]{2,1,0:T(8,128)} %get-tuple-element.57), channel_id=1, source_target_pairs={{1,0},{2,1},{3,2},{4,3},{5,4},{6,5},{7,6},{8,7},{9,8},{10,9},{11,1... | collective-permute-start | bytes 6152 | tf_op jit(solution)/shard_map/ppermute | solution.py:28
  284.6 7.5 %collective-permute-start.46 = (f32[2,256,1]{2,1,0:T(8,128)}, f32[2,256,1]{2,1,0:T(8,128)}, u32[]{:S(2)}, u32[]{:S(2)}) collective-permute-start(f32[2,256,1]{2,1,0:T(8,128)} %get-tuple-element.51), channel_id=1, source_target_pairs={{1,0},{2,1},{3,2},{4,3},{5,4},{6,5},{7,6},{8,7},{9,8},{10,9},{11,1... | collective-permute-start | bytes 6152 | tf_op jit(solution)/shard_map/ppermute | solution.py:28
  302.9 7.7 %collective-permute-start.50 = (f32[2,256,1]{2,1,0:T(8,128)}, f32[2,256,1]{2,1,0:T(8,128)}, u32[]{:S(2)}, u32[]{:S(2)}) collective-permute-start(f32[2,256,1]{2,1,0:T(8,128)} %get-tuple-element.49), channel_id=1, source_target_pairs={{1,0},{2,1},{3,2},{4,3},{5,4},{6,5},{7,6},{8,7},{9,8},{10,9},{11,1... | collective-permute-start | bytes 6152 | tf_op jit(solution)/shard_map/ppermute | solution.py:28
  (203 shorter events, 144.5 us)
Async XLA Ops:
  19.9 45.4 %collective-permute-start.5 = (f32[4,1,32]{2,1,0:T(1,128)S(1)}, f32[4,1,32]{2,1,0:T(1,128)S(1)}, u32[]{:S(2)}, u32[]{:S(2)}) collective-permute-start(f32[4,1,32]{2,1,0:T(1,128)S(1)} %get-tuple-element.78), channel_id=1, source_target_pairs={{0,16},{16,32},{32,48},{48,64},{64,80},{80,96},{96,112},{112,128},... | collective-permute-start | bytes 1544 | tf_op jit(solution)/shard_map/ppermute | solution.py:26
  21.9 51.0 %collective-permute-start.4 = (f32[4,1,32]{2,1,0:T(1,128)S(1)}, f32[4,1,32]{2,1,0:T(1,128)S(1)}, u32[]{:S(2)}, u32[]{:S(2)}) collective-permute-start(f32[4,1,32]{2,1,0:T(1,128)S(1)} %get-tuple-element.77), channel_id=1, source_target_pairs={{16,0},{32,16},{48,32},{64,48},{80,64},{96,80},{112,96},{128,112},... | collective-permute-start | bytes 1544 | tf_op jit(solution)/shard_map/ppermute | solution.py:28
  27.7 47.1 %collective-permute-start.7 = (f32[4,32,1]{2,1,0:T(8,128)S(1)}, f32[4,32,1]{2,1,0:T(8,128)S(1)}, u32[]{:S(2)}, u32[]{:S(2)}) collective-permute-start(f32[4,32,1]{2,1,0:T(8,128)S(1)} %get-tuple-element.76), channel_id=1, source_target_pairs={{0,1},{1,2},{2,3},{3,4},{4,5},{5,6},{6,7},{7,8},{8,9},{9,10},{10,1... | collective-permute-start | bytes 1544 | tf_op jit(solution)/shard_map/ppermute | solution.py:26
  31.5 49.0 %collective-permute-start.6 = (f32[4,32,1]{2,1,0:T(8,128)S(1)}, f32[4,32,1]{2,1,0:T(8,128)S(1)}, u32[]{:S(2)}, u32[]{:S(2)}) collective-permute-start(f32[4,32,1]{2,1,0:T(8,128)S(1)} %get-tuple-element.75), channel_id=1, source_target_pairs={{1,0},{2,1},{3,2},{4,3},{5,4},{6,5},{7,6},{8,7},{9,8},{10,9},{11,1... | collective-permute-start | bytes 1544 | tf_op jit(solution)/shard_map/ppermute | solution.py:28
  38.1 44.5 %collective-permute-start.3 = (f32[2,32,1]{2,1,0:T(8,128)S(1)}, f32[2,32,1]{2,1,0:T(8,128)S(1)}, u32[]{:S(2)}, u32[]{:S(2)}) collective-permute-start(f32[2,32,1]{2,1,0:T(8,128)S(1)} %broadcast.150), channel_id=1, source_target_pairs={{0,1},{1,2},{2,3},{3,4},{4,5},{5,6},{6,7},{7,8},{8,9},{9,10},{10,1... | collective-permute-start | bytes 776 | tf_op jit(solution)/shard_map/ppermute | solution.py:26
  65.3 17.3 %collective-permute-start.2 = (f32[2,32,1]{2,1,0:T(8,128)S(1)}, f32[2,32,1]{2,1,0:T(8,128)S(1)}, u32[]{:S(2)}, u32[]{:S(2)}) collective-permute-start(f32[2,32,1]{2,1,0:T(8,128)S(1)} %broadcast.150), channel_id=1, source_target_pairs={{1,0},{2,1},{3,2},{4,3},{5,4},{6,5},{7,6},{8,7},{9,8},{10,9},{11,1... | collective-permute-start | bytes 776 | tf_op jit(solution)/shard_map/ppermute | solution.py:28
  80.5 112.6 %collective-permute-start.33 = (f32[4,5,256]{1,2,0:T(8,128)}, f32[4,5,256]{1,2,0:T(8,128)S(1)}, u32[]{:S(2)}, u32[]{:S(2)}) collective-permute-start(f32[4,5,256]{1,2,0:T(8,128)} %copy.62), channel_id=1, source_target_pairs={{16,0},{32,16},{48,32},{64,48},{80,64},{96,80},{112,96},{128,112},... | collective-permute-start | bytes 61448 | tf_op jit(solution)/shard_map/ppermute | solution.py:28
  82.8 17.2 %collective-permute-start.9 = (f32[2,1,32]{2,1,0:T(1,128)S(1)}, f32[2,1,32]{2,1,0:T(1,128)S(1)}, u32[]{:S(2)}, u32[]{:S(2)}) collective-permute-start(f32[2,1,32]{2,1,0:T(1,128)S(1)} %get-tuple-element.98), channel_id=1, source_target_pairs={{0,16},{16,32},{32,48},{48,64},{64,80},{80,96},{96,112},{112,128},... | collective-permute-start | bytes 776 | tf_op jit(solution)/shard_map/ppermute | solution.py:26
  101.7 17.6 %collective-permute-start.15 = (f32[2,32,1]{2,1,0:T(8,128)S(1)}, f32[2,32,1]{2,1,0:T(8,128)S(1)}, u32[]{:S(2)}, u32[]{:S(2)}) collective-permute-start(f32[2,32,1]{2,1,0:T(8,128)S(1)} %get-tuple-element.94), channel_id=1, source_target_pairs={{0,1},{1,2},{2,3},{3,4},{4,5},{5,6},{6,7},{7,8},{8,9},{9,10},{10,1... | collective-permute-start | bytes 776 | tf_op jit(solution)/shard_map/ppermute | solution.py:26
  120.7 17.2 %collective-permute-start.17 = (f32[2,1,32]{2,1,0:T(1,128)S(1)}, f32[2,1,32]{2,1,0:T(1,128)S(1)}, u32[]{:S(2)}, u32[]{:S(2)}) collective-permute-start(f32[2,1,32]{2,1,0:T(1,128)S(1)} %get-tuple-element.88), channel_id=1, source_target_pairs={{0,16},{16,32},{32,48},{48,64},{64,80},{80,96},{96,112},{112,128},... | collective-permute-start | bytes 776 | tf_op jit(solution)/shard_map/ppermute | solution.py:26
  139.7 17.6 %collective-permute-start.23 = (f32[2,32,1]{2,1,0:T(8,128)S(1)}, f32[2,32,1]{2,1,0:T(8,128)S(1)}, u32[]{:S(2)}, u32[]{:S(2)}) collective-permute-start(f32[2,32,1]{2,1,0:T(8,128)S(1)} %get-tuple-element.84), channel_id=1, source_target_pairs={{0,1},{1,2},{2,3},{3,4},{4,5},{5,6},{6,7},{7,8},{8,9},{9,10},{10,1... | collective-permute-start | bytes 776 | tf_op jit(solution)/shard_map/ppermute | solution.py:26
  141.6 15.7 %collective-permute-start.22 = (f32[2,32,1]{2,1,0:T(8,128)S(1)}, f32[2,32,1]{2,1,0:T(8,128)S(1)}, u32[]{:S(2)}, u32[]{:S(2)}) collective-permute-start(f32[2,32,1]{2,1,0:T(8,128)S(1)} %get-tuple-element.83), channel_id=1, source_target_pairs={{1,0},{2,1},{3,2},{4,3},{5,4},{6,5},{7,6},{8,7},{9,8},{10,9},{11,1... | collective-permute-start | bytes 776 | tf_op jit(solution)/shard_map/ppermute | solution.py:28
  160.6 17.2 %collective-permute-start.25 = (f32[2,1,256]{2,1,0:T(1,128)S(1)}, f32[2,1,256]{2,1,0:T(1,128)S(1)}, u32[]{:S(2)}, u32[]{:S(2)}) collective-permute-start(f32[2,1,256]{2,1,0:T(1,128)S(1)} %get-tuple-element.72), channel_id=1, source_target_pairs={{0,16},{16,32},{32,48},{48,64},{64,80},{80,96},{96,112},{112,128},... | collective-permute-start | bytes 6152 | tf_op jit(solution)/shard_map/ppermute | solution.py:26
  162.5 17.2 %collective-permute-start.24 = (f32[2,1,256]{2,1,0:T(1,128)S(1)}, f32[2,1,256]{2,1,0:T(1,128)S(1)}, u32[]{:S(2)}, u32[]{:S(2)}) collective-permute-start(f32[2,1,256]{2,1,0:T(1,128)S(1)} %get-tuple-element.71), channel_id=1, source_target_pairs={{16,0},{32,16},{48,32},{64,48},{80,64},{96,80},{112,96},{128,112},... | collective-permute-start | bytes 6152 | tf_op jit(solution)/shard_map/ppermute | solution.py:28
  183.2 34.8 %collective-permute-start.31 = (f32[2,256,1]{2,1,0:T(8,128)}, f32[2,256,1]{2,1,0:T(8,128)}, u32[]{:S(2)}, u32[]{:S(2)}) collective-permute-start(f32[2,256,1]{2,1,0:T(8,128)} %get-tuple-element.68), channel_id=1, source_target_pairs={{0,1},{1,2},{2,3},{3,4},{4,5},{5,6},{6,7},{7,8},{8,9},{9,10},{10,1... | collective-permute-start | bytes 6152 | tf_op jit(solution)/shard_map/ppermute | solution.py:26
  185.1 32.9 %collective-permute-start.30 = (f32[2,256,1]{2,1,0:T(8,128)}, f32[2,256,1]{2,1,0:T(8,128)}, u32[]{:S(2)}, u32[]{:S(2)}) collective-permute-start(f32[2,256,1]{2,1,0:T(8,128)} %get-tuple-element.67), channel_id=1, source_target_pairs={{1,0},{2,1},{3,2},{4,3},{5,4},{6,5},{7,6},{8,7},{9,8},{10,9},{11,1... | collective-permute-start | bytes 6152 | tf_op jit(solution)/shard_map/ppermute | solution.py:28
  222.3 21.6 %collective-permute-start.37 = (f32[2,1,256]{2,1,0:T(1,128)S(1)}, f32[2,1,256]{2,1,0:T(1,128)S(1)}, u32[]{:S(2)}, u32[]{:S(2)}) collective-permute-start(f32[2,1,256]{2,1,0:T(1,128)S(1)} %get-tuple-element.62), channel_id=1, source_target_pairs={{0,16},{16,32},{32,48},{48,64},{64,80},{80,96},{96,112},{112,128},... | collective-permute-start | bytes 6152 | tf_op jit(solution)/shard_map/ppermute | solution.py:26
  224.2 19.7 %collective-permute-start.36 = (f32[2,1,256]{2,1,0:T(1,128)S(1)}, f32[2,1,256]{2,1,0:T(1,128)S(1)}, u32[]{:S(2)}, u32[]{:S(2)}) collective-permute-start(f32[2,1,256]{2,1,0:T(1,128)S(1)} %get-tuple-element.61), channel_id=1, source_target_pairs={{16,0},{32,16},{48,32},{64,48},{80,64},{96,80},{112,96},{128,112},... | collective-permute-start | bytes 6152 | tf_op jit(solution)/shard_map/ppermute | solution.py:28
  248.3 22.4 %collective-permute-start.43 = (f32[2,256,1]{2,1,0:T(8,128)}, f32[2,256,1]{2,1,0:T(8,128)}, u32[]{:S(2)}, u32[]{:S(2)}) collective-permute-start(f32[2,256,1]{2,1,0:T(8,128)} %get-tuple-element.58), channel_id=1, source_target_pairs={{0,1},{1,2},{2,3},{3,4},{4,5},{5,6},{6,7},{7,8},{8,9},{9,10},{10,1... | collective-permute-start | bytes 6152 | tf_op jit(solution)/shard_map/ppermute | solution.py:26
  250.2 20.5 %collective-permute-start.42 = (f32[2,256,1]{2,1,0:T(8,128)}, f32[2,256,1]{2,1,0:T(8,128)}, u32[]{:S(2)}, u32[]{:S(2)}) collective-permute-start(f32[2,256,1]{2,1,0:T(8,128)} %get-tuple-element.57), channel_id=1, source_target_pairs={{1,0},{2,1},{3,2},{4,3},{5,4},{6,5},{7,6},{8,7},{9,8},{10,9},{11,1... | collective-permute-start | bytes 6152 | tf_op jit(solution)/shard_map/ppermute | solution.py:28
  274.9 21.6 %collective-permute-start.45 = (f32[2,1,256]{2,1,0:T(1,128)S(1)}, f32[2,1,256]{2,1,0:T(1,128)S(1)}, u32[]{:S(2)}, u32[]{:S(2)}) collective-permute-start(f32[2,1,256]{2,1,0:T(1,128)S(1)} %get-tuple-element.54), channel_id=1, source_target_pairs={{0,16},{16,32},{32,48},{48,64},{64,80},{80,96},{96,112},{112,128},... | collective-permute-start | bytes 6152 | tf_op jit(solution)/shard_map/ppermute | solution.py:26
  276.9 19.7 %collective-permute-start.44 = (f32[2,1,256]{2,1,0:T(1,128)S(1)}, f32[2,1,256]{2,1,0:T(1,128)S(1)}, u32[]{:S(2)}, u32[]{:S(2)}) collective-permute-start(f32[2,1,256]{2,1,0:T(1,128)S(1)} %get-tuple-element.53), channel_id=1, source_target_pairs={{16,0},{32,16},{48,32},{64,48},{80,64},{96,80},{112,96},{128,112},... | collective-permute-start | bytes 6152 | tf_op jit(solution)/shard_map/ppermute | solution.py:28
  301.0 21.2 %collective-permute-start.51 = (f32[2,256,1]{2,1,0:T(8,128)}, f32[2,256,1]{2,1,0:T(8,128)}, u32[]{:S(2)}, u32[]{:S(2)}) collective-permute-start(f32[2,256,1]{2,1,0:T(8,128)} %get-tuple-element.50), channel_id=1, source_target_pairs={{0,1},{1,2},{2,3},{3,4},{4,5},{5,6},{6,7},{7,8},{8,9},{9,10},{10,1... | collective-permute-start | bytes 6152 | tf_op jit(solution)/shard_map/ppermute | solution.py:26
  302.9 19.3 %collective-permute-start.50 = (f32[2,256,1]{2,1,0:T(8,128)}, f32[2,256,1]{2,1,0:T(8,128)}, u32[]{:S(2)}, u32[]{:S(2)}) collective-permute-start(f32[2,256,1]{2,1,0:T(8,128)} %get-tuple-element.49), channel_id=1, source_target_pairs={{1,0},{2,1},{3,2},{4,3},{5,4},{6,5},{7,6},{8,7},{9,8},{10,9},{11,1... | collective-permute-start | bytes 6152 | tf_op jit(solution)/shard_map/ppermute | solution.py:28
  (50 other events, 686.2 us)
where the time goes:
time: 327 us; the launch traced here: 325 us
  starting transfers between devices  221 us (68%)
  local copies, waits for them, and re-layouts  52.5 us (16%)
  other arithmetic  39.7 us (12%)
  waiting for transfers between devices  7.38 us (2%)
  between operations  4.48 us (1%)
    ppermute x26, starting transfers between devices, extended_2(): lax.ppermute(head, axis, [((i + 1) % count, i) for i in range(ends)])  169 us
    ppermute x26, starting transfers between devices, extended_2(): lax.ppermute(tail, axis, [(i, (i + 1) % count) for i in range(ends)])  52.2 us
    unnamed x52, local copies, waits for them, and re-layouts  12.6 us
    reshape x1, local copies, waits for them, and re-layouts, local(): frame_second.reshape(band_count, coarse_height, FACTOR, coarse_width, FAC...  12.2 us
    reshape x1, local copies, waits for them, and re-layouts, local(): frame_first.reshape(band_count, coarse_height, FACTOR, coarse_width, FACTOR)  11.3 us
    reduce_sum x1, other arithmetic, local(): coarse_second = frame_second.reshape(band_count, coarse_height, FACTOR, c...  7.09 us
    slice x23, local copies, waits for them, and re-layouts, extended_2(): head = lax.slice_in_dim(cells, 0, width, axis=dim)  7.02 us
    reduce_sum x1, other arithmetic, local(): coarse_first = frame_first.reshape(band_count, coarse_height, FACTOR, coa...  7 us
  transfers between devices with their start and end apart: 52, of which 6 were waited for; matrix products, arithmetic and copies ran while one was open for 16% of the time, Pallas kernels for 0%

commit v1 on v0

v1 whole, which is shorter than its diff:
```python
import jax
import jax.numpy as jnp
from jax import lax
from jax.experimental import pallas as pl
from jax.experimental.pallas import tpu as pltpu
from jax.sharding import PartitionSpec as P

FACTOR = 8
TAU = 0.25
SIGMA = 0.25
LAM = 0.3
ALPHA = 0.3
BANDS = 4
T = 256
CT = T // FACTOR
OFF = 16
ROWS = T + 2 * OFF
PANELS = 3
WIDE = 128 * PANELS
CROWS = CT + 16
F32 = jnp.float32
BF16 = jnp.bfloat16
DIRECTIONS = [(-1, -1), (-1, 0), (-1, 1), (0, -1), (0, 1), (1, -1), (1, 0), (1, 1)]


def split3(x):
    hi = x.astype(BF16)
    rest = x - hi.astype(F32)
    mid = rest.astype(BF16)
    low = (rest - mid.astype(F32)).astype(BF16)
    return hi, mid, low


def dot_split(x, w, parts):
    total = None
    for piece in split3(x)[:parts]:
        term = jnp.dot(piece, w, preferred_element_type=F32)
        total = term if total is None else total + term
    return total


def roll(x, amount, axis):
    amount = amount % x.shape[axis]
    return x if amount == 0 else pltpu.roll(x, amount, axis)


def next_minus_prev(x, axis):
    return roll(x, -1, axis) - roll(x, 1, axis)


def following(x):
    return jnp.concatenate([x[1:], x[:1]], axis=0)


def preceding(x):
    return jnp.concatenate([x[-1:], x[:-1]], axis=0)


def across(x):
    lane = lax.broadcasted_iota(jnp.int32, x.shape, 2)
    ahead, behind = roll(x, -1, 2), roll(x, 1, 2)
    return jnp.where(lane == 127, following(ahead), ahead) - jnp.where(lane == 0, preceding(behind), behind)


def shrink(pr, pc):
    return jnp.minimum(1.0, ALPHA * lax.rsqrt(pr * pr + pc * pc))


def kernel(
    f1_ref, f2_ref, sh_ref, flow_ref, coarse_ref,
    s2, f1v, g, q, u, ub, prv, pcv, ti, ce,
    p1, e1, h1, k1, p2, e2, h2, k2,
    local_sem, send_sem, recv_sem,
):
    me_r, me_c = lax.axis_index("row"), lax.axis_index("col")
    n_r, n_c = lax.axis_size("row"), lax.axis_size("col")

    def device(direction):
        dr, dc = direction
        return (lax.rem(me_r + dr + n_r, n_r), lax.rem(me_c + dc + n_c, n_c))

    barrier = pltpu.get_barrier_semaphore()
    for direction in DIRECTIONS:
        pl.semaphore_signal(barrier, inc=1, device_id=device(direction), device_id_type=pl.DeviceIdType.MESH)
    gets = []
    for ref, kept in ((f2_ref, lambda k: s2.at[:, k, pl.ds(OFF, T), :]), (f1_ref, lambda k: f1v.at[:, k])):
        for k in range(2):
            copy = pltpu.make_async_copy(ref.at[:, :, pl.ds(128 * k, 128)], kept(k), local_sem.at[len(gets)])
            copy.start()
            gets.append(copy)

    sends = []

    def send(src, dst, direction):
        slot = len(sends)
        copy = pltpu.make_async_remote_copy(
            src_ref=src, dst_ref=dst, send_sem=send_sem.at[slot], recv_sem=recv_sem.at[slot],
            device_id=device(direction), device_id_type=pl.DeviceIdType.MESH,
        )
        copy.start()
        sends.append(copy)
        return copy

    lane = lax.broadcasted_iota(jnp.int32, (8, 128), 1)
    tall = lax.broadcasted_iota(jnp.int32, (128, 128), 1)
    gets[0].wait()
    gets[1].wait()

    def pack1(i, carry):
        rows = pl.ds(pl.multiple_of(OFF + 8 * i, 8), 8)
        acc = jnp.zeros((8, 128), F32)
        for b in range(BANDS):
            edge = jnp.where(lane < 8, s2[b, 0, rows, :], s2[b, 1, rows, :])
            acc = jnp.where(lane // 16 == b, roll(edge, 16 * b + 8, 1), acc)
        p1[pl.ds(pl.multiple_of(8 * i, 8), 8), :] = acc
        return carry

    lax.fori_loop(0, T // 8, pack1, 0, unroll=4)
    low = p1[0:128, :]
    high = p1[128:256, :]
    odd8 = (tall // 8) % 2 == 1
    e1[0] = jnp.where(odd8, high, roll(low, -8, 1))
    e1[1] = jnp.where(odd8, roll(high, 8, 1), low)
    gets[2].wait()
    gets[3].wait()

    col_id = lax.broadcasted_iota(jnp.int32, (128, 128), 0) // FACTOR
    lane_id = lax.broadcasted_iota(jnp.int32, (128, 128), 1)
    row_sum = (
        lax.broadcasted_iota(jnp.int32, (CT, T), 1) // FACTOR == lax.broadcasted_iota(jnp.int32, (CT, T), 0)
    ).astype(F32).astype(BF16)
    for frame in range(2):
        total = jnp.zeros((T, 128), F32)
        for b in range(BANDS):
            for k in range(2):
                block = f1v[b, k] if frame == 0 else s2[b, k, OFF:OFF + T, :]
                weights = jnp.where(lane_id - CT * b - 16 * k == col_id, 1.0 / 64.0, 0.0).astype(BF16)
                total = total + dot_split(block, weights, 2)
        hi, mid, _ = split3(total)
        ce[1, frame, 8:8 + CT, :] = (
            jnp.dot(row_sum, hi, preferred_element_type=F32) + jnp.dot(row_sum, mid, preferred_element_type=F32)
        )

    pl.semaphore_wait(barrier, len(DIRECTIONS))

    round1 = []
    for direction in DIRECTIONS:
        dr, dc = direction
        src_row = {-1: 8, 0: 8, 1: CT}[dr]
        dst_row = {-1: 8 + CT, 0: 8, 1: 0}[dr]
        count = CT if dr == 0 else 8
        round1.append(send(
            ce.at[1, :, pl.ds(src_row, count), :], ce.at[1 - dc, :, pl.ds(dst_row, count), :], direction
        ) if dc != 0 else send(
            ce.at[1, :, pl.ds(src_row, count), :], ce.at[1, :, pl.ds(dst_row, count), :], direction
        ))
    top, bottom = pl.ds(0, 8), pl.ds(T - 8, 8)
    round1.append(send(s2.at[:, pl.ds(0, 2), pl.ds(OFF, 8)], s2.at[:, pl.ds(0, 2), pl.ds(OFF + T, 8)], (-1, 0)))
    round1.append(send(s2.at[:, pl.ds(0, 2), pl.ds(OFF + T - 8, 8)], s2.at[:, pl.ds(0, 2), pl.ds(OFF - 8, 8)], (1, 0)))
    round1.append(send(e1.at[0], h1.at[0], (0, -1)))
    round1.append(send(e1.at[1], h1.at[1], (0, 1)))
    for dr in (-1, 1):
        for dc in (-1, 1):
            round1.append(send(
                p1.at[top if dr == -1 else bottom, :],
                k1.at[1 if dr == -1 else 0, 1 if dc == -1 else 0], (dr, dc),
            ))
    for copy in round1:
        copy.wait()

    keep_lane = jnp.where(lane[0:1] < 64, jnp.where(me_c == n_c - 1, 0.0, 1.0), jnp.where(me_c == 0, 0.0, 1.0))
    from_right, from_left = h1[0], roll(h1[1], -8, 1)
    for half in range(2):
        mix = jnp.where((tall // 8) % 2 == half, from_right, from_left)
        for b in range(BANDS):
            s2[b, 2, OFF + 128 * half:OFF + 128 * half + 128, :] = roll(mix, -(16 * b + 8 * half), 1) * keep_lane
    for side in range(2):
        mix = jnp.where((lane // 8) % 2 == 0, k1[side, 0], k1[side, 1])
        base = OFF - 8 if side == 0 else OFF + T
        for b in range(BANDS):
            s2[b, 2, base:base + 8, :] = roll(mix, -(16 * b + 8), 1) * keep_lane

    @pl.when(me_r == 0)
    def _():
        s2[:, :, OFF - 8:OFF, :] = jnp.zeros((BANDS, PANELS, 8, 128), F32)

    @pl.when(me_r == n_r - 1)
    def _():
        s2[:, :, OFF + T:OFF + T + 8, :] = jnp.zeros((BANDS, PANELS, 8, 128), F32)

    shift_r, shift_c = sh_ref[0, 0, 0], sh_ref[0, 0, 1]
    amount = jnp.where(shift_c > 0, 128 - shift_c, -shift_c)
    panel_lane = lax.broadcasted_iota(jnp.int32, (PANELS, 8, 128), 2)
    over = panel_lane + shift_c >= 128
    under = panel_lane + shift_c < 0

    def shifted(x):
        turned = pltpu.roll(x, amount, 2)
        return jnp.where(over, following(turned), jnp.where(under, preceding(turned), turned))

    def window(s, carry):
        rows = pl.ds(pl.multiple_of(OFF + 8 * s, 8), 8)
        start = OFF + 8 * s + shift_r
        packed = jnp.zeros((8, 128), F32)
        for b in range(BANDS):
            here = shifted(s2[b, :, pl.ds(start, 8), :])
            down = shifted(s2[b, :, pl.ds(start + 1, 8), :] - s2[b, :, pl.ds(start - 1, 8), :])
            fields = (
                0.5 * down[:2],
                0.5 * across(here)[:2],
                here[:2] - f1v[b, :, pl.ds(pl.multiple_of(8 * s, 8), 8), :],
            )
            for kind in range(3):
                f = BANDS * kind + b
                g[f, 0:2, rows, :] = fields[kind]
                edge = jnp.where(lane < 4, fields[kind][0], fields[kind][1])
                packed = jnp.where(lane // 8 == f, roll(edge, 8 * f + 4, 1), packed)
        p2[pl.ds(pl.multiple_of(8 * s, 8), 8), :] = packed
        return carry

    lax.fori_loop(0, T // 8, window, 0)
    low = p2[0:128, :]
    high = p2[128:256, :]
    odd4 = (tall // 4) % 2 == 1
    e2[0] = jnp.where(odd4, high, roll(low, -4, 1))
    e2[1] = jnp.where(odd4, roll(high, 4, 1), low)

    round2 = [
        send(e2.at[0], h2.at[0], (0, -1)),
        send(e2.at[1], h2.at[1], (0, 1)),
        send(g.at[:, pl.ds(0, 2), pl.ds(OFF, 8)], g.at[:, pl.ds(0, 2), pl.ds(OFF + T, 8)], (-1, 0)),
        send(g.at[:, pl.ds(0, 2), pl.ds(OFF + T - 8, 8)], g.at[:, pl.ds(0, 2), pl.ds(OFF - 8, 8)], (1, 0)),
    ]
    for dr in (-1, 1):
        for dc in (-1, 1):
            round2.append(send(
                p2.at[top if dr == -1 else bottom, :],
                k2.at[1 if dr == -1 else 0, 1 if dc == -1 else 0], (dr, dc),
            ))

    crow = lax.broadcasted_iota(jnp.int32, (CROWS, 128), 0) - 8 + me_r * CT
    clane = lax.broadcasted_iota(jnp.int32, (CROWS, 128), 1)
    ccol = jnp.where(clane < 64, clane, clane - 128) + me_c * CT
    inside = (crow >= 0) & (crow < n_r * CT) & (ccol >= 0) & (ccol < n_c * CT)
    mask = jnp.where(inside, 1.0, 0.0)
    means = []
    for frame in range(2):
        mine, right, left = ce[1, frame], roll(ce[2, frame], CT, 1), roll(ce[0, frame], -CT, 1)
        bands = []
        for b in range(BANDS):
            mix = jnp.where(clane // CT == (b + 1) % 4, right, jnp.where(clane // CT == (b + 3) % 4, left, mine))
            bands.append(roll(mix, -CT * b, 1) * mask)
        means.append(bands)
    grad_r = [0.5 * next_minus_prev(x, 0) for x in means[1]]
    grad_c = [0.5 * next_minus_prev(x, 1) for x in means[1]]
    off = [means[1][b] - means[0][b] for b in range(BANDS)]
    now = [jnp.zeros((CROWS, 128), F32)] * 2
    bar = now
    dual_r, dual_c = list(now), list(now)
    data = [jnp.zeros((CROWS, 128), F32)] * BANDS
    for it in range(3):
        div = [0.0, 0.0]
        if it > 0:
            for c in range(2):
                pr = dual_r[c] + (0.5 * SIGMA) * next_minus_prev(bar[c], 0)
                pc = dual_c[c] + (0.5 * SIGMA) * next_minus_prev(bar[c], 1)
                k = shrink(pr, pc) * mask
                dual_r[c], dual_c[c] = pr * k, pc * k
                div[c] = 0.5 * (next_minus_prev(dual_r[c], 0) + next_minus_prev(dual_c[c], 1))
        pull = [0.0, 0.0]
        for b in range(BANDS):
            rho = off[b]
            if it > 0:
                rho = rho + grad_r[b] * bar[0] + grad_c[b] * bar[1]
            data[b] = jnp.clip(data[b] + SIGMA * rho, -LAM, LAM)
            pull = [pull[0] + data[b] * grad_r[b], pull[1] + data[b] * grad_c[b]]
        later = [(now[c] + TAU * (div[c] - pull[c])) * mask for c in range(2)]
        bar = [2.0 * later[c] - now[c] for c in range(2)]
        now = later
    for c in range(2):
        coarse_ref[c] = now[c][8:8 + CT, 0:CT]

    wide = lax.broadcasted_iota(jnp.int32, (128, WIDE), 1)
    source = jnp.where(wide < T + 64, wide // FACTOR, 128 - (WIDE - wide + FACTOR - 1) // FACTOR)
    spread = jnp.where(lax.broadcasted_iota(jnp.int32, (128, WIDE), 0) == source, float(FACTOR), 0.0).astype(BF16)
    for c in range(2):
        repeated = dot_split(now[c], spread, 3)
        for k in range(PANELS):
            ti[c, k] = repeated[:, 128 * k:128 * k + 128]

    def start_value(c, s):
        return jnp.broadcast_to(ti[c, :, pl.ds(s + 6, 1), :], (PANELS, 8, 128))

    def fill(s, carry):
        rows = pl.ds(pl.multiple_of(8 * s, 8), 8)
        for c in range(2):
            value = start_value(c, s)
            u[c, :, rows, :] = value
            ub[c, :, rows, :] = value
        return carry

    lax.fori_loop(1, ROWS // 8 - 1, fill, 0)

    for copy in round2:
        copy.wait()
    from_right, from_left = h2[0], roll(h2[1], -4, 1)
    for half in range(2):
        mix = jnp.where((tall // 4) % 2 == half, from_right, from_left)
        for f in range(3 * BANDS):
            g[f, 2, OFF + 128 * half:OFF + 128 * half + 128, :] = roll(mix, -(8 * f + 4 * half), 1)
    for side in range(2):
        mix = jnp.where((lane // 4) % 2 == 0, k2[side, 0], k2[side, 1])
        base = OFF - 8 if side == 0 else OFF + T
        for f in range(3 * BANDS):
            g[f, 2, base:base + 8, :] = roll(mix, -(8 * f + 4), 1)

    flane = panel_lane + 128 * lax.broadcasted_iota(jnp.int32, (PANELS, 8, 128), 0)
    fcol = jnp.where(flane < T + 64, flane, flane - WIDE) + me_c * T
    col_mask = jnp.where((fcol >= 0) & (fcol < n_c * T), 1.0, 0.0)

    def strip_mask(s):
        row = 8 * s - OFF + me_r * T
        return col_mask * jnp.where((row >= 0) & (row < n_r * T), 1.0, 0.0)

    for it in range(3):
        def dual(s, carry):
            base = 8 * s
            rows = pl.ds(pl.multiple_of(base, 8), 8)
            m = strip_mask(s)
            for c in range(2):
                pr = (0.5 * SIGMA) * (ub[c, :, pl.ds(base + 1, 8), :] - ub[c, :, pl.ds(base - 1, 8), :])
                pc = (0.5 * SIGMA) * across(ub[c, :, rows, :])
                if it > 0:
                    pr = prv[c, :, rows, :] + pr
                    pc = pcv[c, :, rows, :] + pc
                k = shrink(pr, pc) * m
                prv[c, :, rows, :] = pr * k
                pcv[c, :, rows, :] = pc * k
            return carry

        lax.fori_loop(1, ROWS // 8 - 1, dual, 0)

        def primal(s, carry):
            base = 8 * s
            rows = pl.ds(pl.multiple_of(base, 8), 8)
            m = strip_mask(s)
            if it > 0:
                step = [ub[c, :, rows, :] - start_value(c, s) for c in range(2)]
            pull = [0.0, 0.0]
            for b in range(BANDS):
                gr, gc, rho = g[b, :, rows, :], g[BANDS + b, :, rows, :], g[2 * BANDS + b, :, rows, :]
                if it > 0:
                    rho = q[b, :, rows, :] + SIGMA * (rho + gr * step[0] + gc * step[1])
                else:
                    rho = SIGMA * rho
                dq = jnp.clip(rho, -LAM, LAM)
                if it < 2:
                    q[b, :, rows, :] = dq
                pull = [pull[0] + dq * gr, pull[1] + dq * gc]
            for c in range(2):
                div = 0.5 * (
                    prv[c, :, pl.ds(base + 1, 8), :] - prv[c, :, pl.ds(base - 1, 8), :]
                    + across(pcv[c, :, rows, :])
                )
                was = u[c, :, rows, :]
                later = (was + TAU * (div - pull[c])) * m
                if it < 2:
                    u[c, :, rows, :] = later
                    ub[c, :, rows, :] = 2.0 * later - was
                else:
                    out_rows = pl.ds(pl.multiple_of(base - OFF, 8), 8)
                    for k in range(2):
                        flow_ref[c, out_rows, 128 * k:128 * k + 128] = later[k]
            return carry

        if it < 2:
            lax.fori_loop(1, ROWS // 8 - 1, primal, 0)
        else:
            lax.fori_loop(OFF // 8, (OFF + T) // 8, primal, 0)


def local(frame_first, frame_second, shifts):
    vmem = pltpu.VMEM
    return pl.pallas_call(
        kernel,
        out_shape=(
            jax.ShapeDtypeStruct((2, T, T), F32),
            jax.ShapeDtypeStruct((2, CT, CT), F32),
        ),
        in_specs=[
            pl.BlockSpec(memory_space=pl.ANY),
            pl.BlockSpec(memory_space=pl.ANY),
            pl.BlockSpec(memory_space=pltpu.SMEM),
        ],
        out_specs=(pl.BlockSpec(memory_space=vmem), pl.BlockSpec(memory_space=vmem)),
        scratch_shapes=[
            vmem((BANDS, PANELS, ROWS, 128), F32),
            vmem((BANDS, 2, T, 128), F32),
            vmem((3 * BANDS, PANELS, ROWS, 128), F32),
            vmem((BANDS, PANELS, ROWS, 128), F32),
            vmem((2, PANELS, ROWS, 128), F32),
            vmem((2, PANELS, ROWS, 128), F32),
            vmem((2, PANELS, ROWS, 128), F32),
            vmem((2, PANELS, ROWS, 128), F32),
            vmem((2, PANELS, CROWS, 128), F32),
            vmem((3, 2, CROWS, 128), F32),
            vmem((T, 128), F32), vmem((2, 128, 128), F32), vmem((2, 128, 128), F32), vmem((2, 2, 8, 128), F32),
            vmem((T, 128), F32), vmem((2, 128, 128), F32), vmem((2, 128, 128), F32), vmem((2, 2, 8, 128), F32),
            pltpu.SemaphoreType.DMA((4,)),
            pltpu.SemaphoreType.DMA((24,)),
            pltpu.SemaphoreType.DMA((24,)),
        ],
        compiler_params=pltpu.CompilerParams(
            collective_id=0, has_side_effects=True, vmem_limit_bytes=48 * 1024 * 1024
        ),
    )(frame_first, frame_second, shifts)


def solution(mesh):
    return jax.shard_map(
        local,
        mesh=mesh,
        in_specs=(P(None, "row", "col"), P(None, "row", "col"), P("row", "col", None)),
        out_specs=(P(None, "row", "col"), P(None, "row", "col")),
        check_vma=False,
    )
```

time: 327 us -> 57.3 us (0.18)
  the two profiles are of different devices: /device:TPU:24 before, /device:TPU:1 now
where the time goes in v1:
time: 57.3 us; the launch traced here: 57.2 us
  Pallas kernels  52 us (91%)
  local copies, waits for them, and re-layouts  4.51 us (8%)
  between operations  0.65 us (1%)
    pallas_call x1, Pallas kernels, local(): pl.pallas_call(kernel, out_shape=(jax.ShapeDtypeStruct((2, T, T), F32), j...  52 us
    unnamed x8, local copies, waits for them, and re-layouts  4.51 us

profile of v1, /device:TPU:1, one launch (start us, length us, event | category | flops | bytes accessed | tf_op | source)
XLA Modules:
  0.0 57.2 jit_solution(2679797938672430655)
XLA Ops:
  0.6 0.0 copy-start
  0.6 1.2 %copy-done = f32[4,256,256]{2,1,0:T(8,128)S(1)} copy-done((f32[4,256,256]{2,1,0:T(8,128)S(1)}, f32[4,256,256]{2,1,0:T(8,128)}, u32[]{:S(2)}) %copy-start) | copy-done | bytes 1048600
  1.9 0.0 copy-start.1
  1.9 1.2 %copy-done.1 = f32[4,256,256]{2,1,0:T(8,128)S(1)} copy-done((f32[4,256,256]{2,1,0:T(8,128)S(1)}, f32[4,256,256]{2,1,0:T(8,128)}, u32[]{:S(2)}) %copy-start.1) | copy-done | bytes 1048600
  3.1 0.0 copy-start.2
  3.1 0.7 %copy-done.2 = s32[1,1,2]{2,1,0:T(1,128)S(1)} copy-done((s32[1,1,2]{2,1,0:T(1,128)S(1)}, s32[1,1,2]{2,1,0:T(1,128)}, u32[]{:S(2)}) %copy-start.2) | copy-done | bytes 32
  3.7 52.0 %shard_map.50 = (f32[2,256,256]{2,1,0:T(8,128)S(1)}, f32[2,32,32]{2,1,0:T(8,128)S(1)}) custom-call(f32[4,256,256]{2,1,0:T(8,128)S(1)} %copy-done, f32[4,256,256]{2,1,0:T(8,128)S(1)} %copy-done.1, s32[1,1,2]{2,1,0:T(1,128)S(1)} %copy-done.2), custom_call_target="tpu_custom_call" | custom-call | tf_op jit(solution)/shard_map/pallas_call | solution.py:384
  55.8 0.8 %copy.7 = f32[2,256,256]{2,1,0:T(8,128)} copy(f32[2,256,256]{2,1,0:T(8,128)S(1)} %get-tuple-element.4) | data formatting | bytes 1048576
  56.6 0.6 %copy.8 = f32[2,32,32]{2,1,0:T(8,128)} copy(f32[2,32,32]{2,1,0:T(8,128)S(1)} %get-tuple-element.5) | data formatting | bytes 16384
Async XLA Ops:
  0.6 1.2 %copy-start = (f32[4,256,256]{2,1,0:T(8,128)S(1)}, f32[4,256,256]{2,1,0:T(8,128)}, u32[]{:S(2)}) copy-start(f32[4,256,256]{2,1,0:T(8,128)} %f1_ref.1) | copy-start | bytes 3145732
  1.9 1.2 %copy-start.1 = (f32[4,256,256]{2,1,0:T(8,128)S(1)}, f32[4,256,256]{2,1,0:T(8,128)}, u32[]{:S(2)}) copy-start(f32[4,256,256]{2,1,0:T(8,128)} %f2_ref.1) | copy-start | bytes 3145732
  3.1 0.7 %copy-start.2 = (s32[1,1,2]{2,1,0:T(1,128)S(1)}, s32[1,1,2]{2,1,0:T(1,128)}, u32[]{:S(2)}) copy-start(s32[1,1,2]{2,1,0:T(1,128)} %sh_ref.1) | copy-start | bytes 28

commit v2 on v1

v2 whole, which is shorter than its diff:
```python
import jax
import jax.numpy as jnp
from jax import lax
from jax.experimental import pallas as pl
from jax.experimental.pallas import tpu as pltpu
from jax.sharding import PartitionSpec as P

FACTOR = 8
TAU = 0.25
SIGMA = 0.25
LAM = 0.3
ALPHA = 0.3
BANDS = 4
T = 256
CT = T // FACTOR
OFF = 24
ROWS = T + 2 * OFF
FIRST = OFF - 8
STRIPS = T // 8 + 2
UNROLL = STRIPS // 2
PANELS = 3
DEEP = 9
THIN = 4
CROWS = CT + 16
F32 = jnp.float32
BF16 = jnp.bfloat16
DIRECTIONS = [(-1, -1), (-1, 1), (1, -1), (1, 1), (0, -1), (0, 1), (-1, 0), (1, 0)]


def split3(x):
    hi = x.astype(BF16)
    rest = x - hi.astype(F32)
    mid = rest.astype(BF16)
    low = (rest - mid.astype(F32)).astype(BF16)
    return hi, mid, low


def dot_split(x, w, parts):
    total = None
    for piece in split3(x)[:parts]:
        term = jnp.dot(piece, w, preferred_element_type=F32)
        total = term if total is None else total + term
    return total


def roll(x, amount, axis):
    amount = amount % x.shape[axis]
    return x if amount == 0 else pltpu.roll(x, amount, axis)


def next_minus_prev(x, axis):
    return roll(x, -1, axis) - roll(x, 1, axis)


def following(x):
    return jnp.concatenate([x[1:], x[:1]], axis=0)


def preceding(x):
    return jnp.concatenate([x[-1:], x[:-1]], axis=0)


def across(x):
    lane = lax.broadcasted_iota(jnp.int32, x.shape, 2)
    ahead, behind = roll(x, -1, 2), roll(x, 1, 2)
    return jnp.where(lane == 127, following(ahead), ahead) - jnp.where(lane == 0, preceding(behind), behind)


def shrink(square):
    return jnp.minimum(1.0, ALPHA * lax.rsqrt(square))


def aligned(start, size=8):
    return pl.ds(pl.multiple_of(start, 8), size)


def kernel(
    f1_ref, f2_ref, sh_ref, flow_ref, coarse_ref,
    s2, f1v, g, a, p1, u, ub, prv, pcv, tc, ce, cs, cr,
    pack, es, er, kr, eq, own, shs, shr,
    local_sem, send_sem, recv_sem,
):
    me_r, me_c = lax.axis_index("row"), lax.axis_index("col")
    n_r, n_c = lax.axis_size("row"), lax.axis_size("col")

    def device(direction):
        dr, dc = direction
        return (lax.rem(me_r + dr + n_r, n_r), lax.rem(me_c + dc + n_c, n_c))

    barrier = pltpu.get_barrier_semaphore()
    for direction in DIRECTIONS:
        pl.semaphore_signal(barrier, inc=1, device_id=device(direction), device_id_type=pl.DeviceIdType.MESH)
    gets = []
    for ref, kept in ((f2_ref, s2), (f1_ref, f1v)):
        for k in range(2):
            copy = pltpu.make_async_copy(
                ref.at[:, :, pl.ds(128 * k, 128)], kept.at[:, k, pl.ds(OFF, T), :], local_sem.at[len(gets)]
            )
            copy.start()
            gets.append(copy)
    my_shift = (sh_ref[0, 0, 0], sh_ref[0, 0, 1])
    sub8 = lax.broadcasted_iota(jnp.int32, (8, 128), 0)
    shs[...] = jnp.where(sub8 == 0, my_shift[0], my_shift[1])

    sends = []

    def send(src, dst, direction):
        slot = len(sends)
        copy = pltpu.make_async_remote_copy(
            src_ref=src, dst_ref=dst, send_sem=send_sem.at[slot], recv_sem=recv_sem.at[slot],
            device_id=device(direction), device_id_type=pl.DeviceIdType.MESH,
        )
        copy.start()
        sends.append(copy)

    lane = lax.broadcasted_iota(jnp.int32, (8, 128), 1)
    place = lane % 16
    right_side = lane < 64
    tall = lax.broadcasted_iota(jnp.int32, (T // 2, 128), 1) < 64
    for copy in gets:
        copy.wait()

    def packing(i, carry):
        rows = aligned(OFF + 8 * i)
        acc = jnp.zeros((8, 128), F32)
        for b in range(BANDS):
            left2, right2, left1, right1 = s2[b, 0, rows, :], s2[b, 1, rows, :], f1v[b, 0, rows, :], f1v[b, 1, rows, :]
            left = jnp.where(place < 6, roll(left1, 16 * b, 1), roll(left2, 16 * b + 6, 1))
            right = jnp.where(place < 10, roll(right2, 16 * b + 74, 1), roll(right1, 16 * b + 78, 1))
            acc = jnp.where(lane // 16 == b, left, jnp.where(lane // 16 == b + 4, right, acc))
        pack[aligned(8 * i), :] = acc
        return carry

    lax.fori_loop(0, T // 8, packing, 0, unroll=8)
    upper, lower = pack[0:128, :], pack[128:256, :]
    es[0] = jnp.where(tall, upper, roll(lower, 64, 1))
    es[1] = jnp.where(tall, roll(upper, 64, 1), lower)

    col_id = lax.broadcasted_iota(jnp.int32, (128, 128), 0) // FACTOR
    lane_id = lax.broadcasted_iota(jnp.int32, (128, 128), 1)
    row_sum = (
        lax.broadcasted_iota(jnp.int32, (CT, T), 1) // FACTOR == lax.broadcasted_iota(jnp.int32, (CT, T), 0)
    ).astype(F32).astype(BF16)
    for frame in range(2):
        total = jnp.zeros((T, 128), F32)
        for b in range(BANDS):
            for k in range(2):
                block = (f1v if frame == 0 else s2)[b, k, OFF:OFF + T, :]
                weights = jnp.where(lane_id - CT * b - 16 * k == col_id, 1.0 / 64.0, 0.0).astype(BF16)
                total = total + dot_split(block, weights, 2)
        hi, mid, _ = split3(total)
        ce[frame, 8:8 + CT, :] = (
            jnp.dot(row_sum, hi, preferred_element_type=F32) + jnp.dot(row_sum, mid, preferred_element_type=F32)
        )
    group = (lax.broadcasted_iota(jnp.int32, (16, 128), 1) % CT) // 8
    edge_l = edge_r = jnp.zeros((16, 128), F32)
    for frame in range(2):
        for half in range(2):
            n = 2 * frame + half
            piece = ce[frame, 8 + 16 * half:24 + 16 * half, :]
            edge_l = jnp.where(group == n, roll(piece, 8 * n, 1), edge_l)
            edge_r = jnp.where(group == n, roll(piece, 8 * n - 24, 1), edge_r)
    cs[0] = edge_l
    cs[1] = edge_r

    pl.semaphore_wait(barrier, len(DIRECTIONS))

    def send_rows(dr, dc, seen):
        for frame in range(2):
            send(
                ce.at[frame, pl.ds(8 if dr < 0 else CT, 8), :], cr.at[seen, pl.ds(8 * frame, 8), :], (dr, dc)
            )

    for dr, dc in DIRECTIONS:
        seen = DIRECTIONS.index((-dr, -dc))
        if dr != 0 and dc != 0:
            send(pack.at[pl.ds(0 if dr < 0 else T - 16, 16), :], kr.at[seen], (dr, dc))
            send_rows(dr, dc, seen)
        elif dr == 0:
            side = 0 if dc < 0 else 1
            send(es.at[side], er.at[side], (dr, dc))
            send(cs.at[side], cr.at[seen], (dr, dc))
        else:
            send_rows(dr, dc, seen)
            from2, to2 = (OFF, OFF + T) if dr < 0 else (OFF + T - DEEP, OFF - DEEP)
            from1, to1 = (OFF, OFF + T) if dr < 0 else (OFF + T - THIN, OFF - THIN)
            both = pl.ds(0, 2)
            send(s2.at[:, both, pl.ds(from2, DEEP), :], s2.at[:, both, pl.ds(to2, DEEP), :], (dr, dc))
            send(f1v.at[:, both, pl.ds(from1, THIN), :], f1v.at[:, both, pl.ds(to1, THIN), :], (dr, dc))
        send(shs, shr.at[seen], (dr, dc))

    def own_edge(start):
        acc = jnp.zeros((8, 128), F32)
        for b in range(BANDS):
            left, right = s2[b, 0, aligned(start), :], s2[b, 1, aligned(start), :]
            acc = jnp.where(lane // 16 == b, roll(right, 16 * b + 6, 1), acc)
            acc = jnp.where(lane // 16 == b + 4, roll(left, 16 * b + 74, 1), acc)
        return acc

    def owning(i, carry):
        own[aligned(OFF + 8 * i), :] = own_edge(OFF + 8 * i)
        return carry

    lax.fori_loop(0, T // 8, owning, 0, unroll=8)

    for copy in sends:
        copy.wait()

    def at(direction):
        return DIRECTIONS.index(direction)

    shift_at = {d: (shr[at(d), 0, 0], shr[at(d), 1, 0]) for d in DIRECTIONS}

    keep_lane = jnp.where(
        lane[0:1] < 64, jnp.where(me_c == n_c - 1, 0.0, 1.0), jnp.where(me_c == 0, 0.0, 1.0)
    )
    eq[OFF:OFF + 128, :] = jnp.where(tall, er[0], roll(er[1], 64, 1)) * keep_lane
    eq[OFF + 128:OFF + 256, :] = jnp.where(tall, roll(er[0], 64, 1), er[1]) * keep_lane
    side16 = lax.broadcasted_iota(jnp.int32, (16, 128), 1) < 64
    eq[OFF - 16:OFF, :] = jnp.where(side16, kr[at((-1, 1))], kr[at((-1, -1))]) * keep_lane
    eq[OFF + T:OFF + T + 16, :] = jnp.where(side16, kr[at((1, 1))], kr[at((1, -1))]) * keep_lane

    @pl.when(me_r == 0)
    def _():
        s2[:, 0:2, OFF - 16:OFF, :] = jnp.zeros((BANDS, 2, 16, 128), F32)
        eq[OFF - 16:OFF, :] = jnp.zeros((16, 128), F32)

    @pl.when(me_r == n_r - 1)
    def _():
        s2[:, 0:2, OFF + T:OFF + T + 16, :] = jnp.zeros((BANDS, 2, 16, 128), F32)
        eq[OFF + T:OFF + T + 16, :] = jnp.zeros((16, 128), F32)

    for start in (OFF - 16, OFF - 8, OFF + T, OFF + T + 8):
        own[start:start + 8, :] = own_edge(start)

    theirs = (right_side & (place >= 6)) | ((lane >= 64) & (place < 10))

    def third(i, carry):
        rows = aligned(OFF - 16 + 8 * i)
        x = eq[rows, :]
        mix = jnp.where((place >= 6) & (place < 13), x, roll(x, 60, 1))
        for b in range(BANDS):
            s2[b, 2, rows, :] = roll(mix, -(16 * b + 6), 1)
        own[rows, :] = jnp.where(theirs, x, own[rows, :])
        return carry

    lax.fori_loop(0, STRIPS + 2, third, 0, unroll=9)

    panel_lane = lax.broadcasted_iota(jnp.int32, (PANELS, 8, 128), 2)

    def back(shift):
        return jnp.where(shift > 0, 128 - shift, -shift)

    def store_data(fields, b, panels, rows, pull):
        dr, dc, wf = fields
        first = jnp.clip(wf, -LAM, LAM)
        g[b, panels, rows, :] = dr
        g[BANDS + b, panels, rows, :] = dc
        g[2 * BANDS + b, panels, rows, :] = wf
        a[b, panels, rows, :] = first + wf
        return [pull[0] + first * dr, pull[1] + first * dc]

    def window(base, shift):
        rows = aligned(base)
        start = base + shift[0]
        amount = back(shift[1])
        over = panel_lane + shift[1] >= 128
        under = panel_lane + shift[1] < 0

        def shifted(x):
            turned = pltpu.roll(x, amount, 2)
            return jnp.where(over, following(turned), jnp.where(under, preceding(turned), turned))

        pull = [0.0, 0.0]
        for b in range(BANDS):
            here = shifted(s2[b, :, pl.ds(start, 8), :])
            down = shifted(s2[b, :, pl.ds(start + 1, 8), :] - s2[b, :, pl.ds(start - 1, 8), :])
            fields = (down[:2], across(here)[:2], SIGMA * (here[:2] - f1v[b, :, rows, :]))
            pull = store_data(fields, b, slice(0, 2), rows, pull)
        for c in range(2):
            p1[c, 0:2, rows, :] = pull[c]

    def window_loop(i, carry):
        window(OFF + 8 * i, my_shift)
        return carry

    lax.fori_loop(0, T // 8, window_loop, 0, unroll=4)
    window(OFF - 8, shift_at[(-1, 0)])
    window(OFF + T, shift_at[(1, 0)])

    def edge(base, right, left):
        rows = aligned(base)

        def pick(x, y):
            return jnp.where(right_side, pltpu.roll(x, back(right[1]), 1), pltpu.roll(y, back(left[1]), 1))

        def near(shift, step):
            return own[pl.ds(base + shift[0] + step, 8), :]

        here = pick(near(right, 0), near(left, 0))
        down = pick(near(right, 1) - near(right, -1), near(left, 1) - near(left, -1))
        x = eq[rows, :]
        first = jnp.where(right_side, roll(x, 6, 1), roll(x, -4, 1))
        kinds = []
        for field in (down, next_minus_prev(here, 1), SIGMA * (here - first)):
            kinds.append(jnp.where((place >= 6) & (place < 10), field, roll(field, 60, 1)))
        pull = [0.0, 0.0]
        for b in range(BANDS):
            fields = [roll(kind, -(16 * b + 6), 1) for kind in kinds]
            pull = store_data(fields, b, 2, rows, pull)
        for c in range(2):
            p1[c, 2, rows, :] = pull[c]

    def edge_loop(i, carry):
        edge(OFF + 8 * i, shift_at[(0, 1)], shift_at[(0, -1)])
        return carry

    lax.fori_loop(0, T // 8, edge_loop, 0, unroll=8)
    edge(OFF - 8, shift_at[(-1, 1)], shift_at[(-1, -1)])
    edge(OFF + T, shift_at[(1, 1)], shift_at[(1, -1)])

    crow = lax.broadcasted_iota(jnp.int32, (CROWS, 128), 0) - 8 + me_r * CT
    clane = lax.broadcasted_iota(jnp.int32, (CROWS, 128), 1)
    ccol = jnp.where(clane < 64, clane, clane - 128) + me_c * CT
    mask = jnp.where((crow >= 0) & (crow < n_r * CT) & (ccol >= 0) & (ccol < n_c * CT), 1.0, 0.0)
    means = []
    for frame in range(2):
        def column(dc):
            parts = [cr[at((-1, dc)), 8 * frame:8 * frame + 8, :]]
            turn = CT * dc
            if dc == 0:
                parts.append(ce[frame, 8:8 + CT, :])
            else:
                for half in range(2):
                    n = 2 * frame + half
                    parts.append(roll(cr[at((0, dc))], (0 if dc > 0 else 24) - 8 * n, 1))
            parts.append(cr[at((1, dc)), 8 * frame:8 * frame + 8, :])
            return roll(jnp.concatenate(parts, axis=0), turn, 1)

        mine, right, left = column(0), column(1), column(-1)
        bands = []
        for b in range(BANDS):
            mix = jnp.where(clane // CT == (b + 1) % 4, right, jnp.where(clane // CT == (b + 3) % 4, left, mine))
            bands.append(roll(mix, -CT * b, 1) * mask)
        means.append(bands)
    grad_r = [0.5 * next_minus_prev(x, 0) for x in means[1]]
    grad_c = [0.5 * next_minus_prev(x, 1) for x in means[1]]
    off = [means[1][b] - means[0][b] for b in range(BANDS)]
    now = [jnp.zeros((CROWS, 128), F32)] * 2
    bar = now
    dual_r, dual_c = list(now), list(now)
    data = [jnp.zeros((CROWS, 128), F32)] * BANDS
    for it in range(3):
        div = [0.0, 0.0]
        if it > 0:
            for c in range(2):
                pr = dual_r[c] + (0.5 * SIGMA) * next_minus_prev(bar[c], 0)
                pc = dual_c[c] + (0.5 * SIGMA) * next_minus_prev(bar[c], 1)
                k = shrink(pr * pr + pc * pc) * mask
                dual_r[c], dual_c[c] = pr * k, pc * k
                div[c] = 0.5 * (next_minus_prev(dual_r[c], 0) + next_minus_prev(dual_c[c], 1))
        pull = [0.0, 0.0]
        for b in range(BANDS):
            rho = off[b]
            if it > 0:
                rho = rho + grad_r[b] * bar[0] + grad_c[b] * bar[1]
            data[b] = jnp.clip(data[b] + SIGMA * rho, -LAM, LAM)
            pull = [pull[0] + data[b] * grad_r[b], pull[1] + data[b] * grad_c[b]]
        later = [(now[c] + TAU * (div[c] - pull[c])) * mask for c in range(2)]
        bar = [2.0 * later[c] - now[c] for c in range(2)]
        now = later
    for c in range(2):
        coarse_ref[c] = now[c][8:8 + CT, 0:CT]

    wide_shape = (128, 128 * PANELS)
    wide = lax.broadcasted_iota(jnp.int32, wide_shape, 1)
    source = jnp.where(wide < T + 64, wide // FACTOR, 128 - (128 * PANELS - wide + FACTOR - 1) // FACTOR)
    spread = jnp.where(lax.broadcasted_iota(jnp.int32, wide_shape, 0) == source, 1.0, 0.0).astype(BF16)
    block_lane = lax.broadcasted_iota(jnp.int32, (PANELS, CROWS, 128), 2)
    block_lane = block_lane + 128 * lax.broadcasted_iota(jnp.int32, (PANELS, CROWS, 128), 0)
    block_row = lax.broadcasted_iota(jnp.int32, (PANELS, CROWS, 128), 1) - 8 + me_r * CT
    block_col = jnp.where(block_lane < T + 64, block_lane, block_lane - 128 * PANELS) + me_c * T
    block_mask = jnp.where(
        (block_row >= 0) & (block_row < n_r * CT) & (block_col >= 0) & (block_col < n_c * T), 1.0, 0.0
    )
    for c in range(2):
        repeated = dot_split(now[c], spread, 3)
        t = jnp.stack([repeated[:, 128 * k:128 * k + 128] for k in range(PANELS)])
        first_r = t - roll(t, 1, 1)
        last_r = roll(t, -1, 1) - t
        step_c = across(t)
        square = step_c * step_c
        k_first = shrink(first_r * first_r + square) * block_mask
        k_inner = shrink(square) * block_mask
        k_last = shrink(last_r * last_r + square) * block_mask
        pr_first, pr_last = first_r * k_first, last_r * k_last
        pc_first, pc_inner, pc_last = step_c * k_first, step_c * k_inner, step_c * k_last
        inner = across(pc_inner)
        for n, value in enumerate((
            t, pr_first, pr_last, pc_first, pc_inner, pc_last,
            across(pc_first) - roll(pr_last, 1, 1), inner - pr_first, inner, inner + pr_last,
            across(pc_last) + roll(pr_first, -1, 1),
        )):
            tc[n, c] = value

    def block_row_of(n, c, s):
        return jnp.broadcast_to(tc[n, c, :, pl.ds(s + 7, 1), :], (PANELS, 8, 128))

    panel_sub = lax.broadcasted_iota(jnp.int32, (PANELS, 8, 128), 1)
    right_in = jnp.where(me_c == n_c - 1, 0.0, 1.0)
    left_in = jnp.where(me_c == 0, 0.0, 1.0)
    col_mask = jnp.where(panel_lane[:1] < 64, right_in, left_in)

    def inside_cols(x):
        return jnp.concatenate([x[:2], x[2:] * col_mask], axis=0)

    def clear_rows(ref):
        @pl.when(me_r == 0)
        def _():
            ref[:, :, FIRST:FIRST + 8, :] = jnp.zeros((2, PANELS, 8, 128), F32)

        @pl.when(me_r == n_r - 1)
        def _():
            ref[:, :, OFF + T:OFF + T + 8, :] = jnp.zeros((2, PANELS, 8, 128), F32)

    def opening(s, carry):
        rows = aligned(FIRST + 8 * s)
        for c in range(2):
            t, pr_first, pr_last, pc_first, pc_inner, pc_last, d0, d1, dm, d6, d7 = [
                block_row_of(n, c, s) for n in range(11)
            ]
            at0, at7 = panel_sub == 0, panel_sub == 7
            div = jnp.where(at0, d0, jnp.where(at7, d7, jnp.where(panel_sub == 1, d1, jnp.where(panel_sub == 6, d6, dm))))
            prv[c, :, rows, :] = jnp.where(at0, pr_first, jnp.where(at7, pr_last, 0.0))
            pcv[c, :, rows, :] = jnp.where(at0, pc_first, jnp.where(at7, pc_last, pc_inner))
            later = t + (1.0 / 64.0) * (div - p1[c, :, rows, :])
            u[c, :, rows, :] = later
            ub[c, :, rows, :] = inside_cols(2.0 * later - t)
        return carry

    lax.fori_loop(0, STRIPS, opening, 0, unroll=UNROLL)
    clear_rows(ub)

    for it in (1, 2):
        def dual(s, carry):
            base = FIRST + 8 * s
            rows = aligned(base)
            for c in range(2):
                pr = prv[c, :, rows, :] + (ub[c, :, pl.ds(base + 1, 8), :] - ub[c, :, pl.ds(base - 1, 8), :])
                pc = pcv[c, :, rows, :] + across(ub[c, :, rows, :])
                k = inside_cols(shrink(pr * pr + pc * pc))
                prv[c, :, rows, :] = pr * k
                pcv[c, :, rows, :] = pc * k
            return carry

        lax.fori_loop(0, STRIPS, dual, 0, unroll=UNROLL)
        clear_rows(prv)

        def primal(s, carry):
            base = FIRST + 8 * s
            rows = aligned(base)
            n = PANELS if it < 2 else 2
            step = [(ub[c, :, rows, :] - block_row_of(0, c, s))[:n] for c in range(2)]
            pull = [0.0, 0.0]
            for b in range(BANDS):
                gr, gc = g[b, 0:n, rows, :], g[BANDS + b, 0:n, rows, :]
                value = a[b, 0:n, rows, :] + gr * step[0] + gc * step[1]
                if it == 2:
                    value = value + g[2 * BANDS + b, 0:n, rows, :]
                value = jnp.clip(value, -LAM, LAM)
                if it < 2:
                    a[b, :, rows, :] = value
                pull = [pull[0] + value * gr, pull[1] + value * gc]
            for c in range(2):
                div = (
                    prv[c, 0:n, pl.ds(base + 1, 8), :] - prv[c, 0:n, pl.ds(base - 1, 8), :]
                    + across(pcv[c, :, rows, :])[:n]
                )
                was = u[c, 0:n, rows, :]
                later = was + (1.0 / 64.0) * (div - pull[c])
                if it < 2:
                    u[c, :, rows, :] = later
                    ub[c, :, rows, :] = inside_cols(2.0 * later - was)
                else:
                    for k in range(2):
                        flow_ref[c, aligned(base - OFF), 128 * k:128 * k + 128] = 8.0 * later[k]
            return carry

        if it < 2:
            lax.fori_loop(0, STRIPS, primal, 0, unroll=UNROLL)
            clear_rows(ub)
        else:
            lax.fori_loop(1, STRIPS - 1, primal, 0, unroll=8)


def local(frame_first, frame_second, shifts):
    vmem = pltpu.VMEM
    field = vmem((2, PANELS, ROWS, 128), F32)
    return pl.pallas_call(
        kernel,
        out_shape=(
            jax.ShapeDtypeStruct((2, T, T), F32),
            jax.ShapeDtypeStruct((2, CT, CT), F32),
        ),
        in_specs=[
            pl.BlockSpec(memory_space=pl.ANY),
            pl.BlockSpec(memory_space=pl.ANY),
            pl.BlockSpec(memory_space=pltpu.SMEM),
        ],
        out_specs=(pl.BlockSpec(memory_space=vmem), pl.BlockSpec(memory_space=vmem)),
        scratch_shapes=[
            vmem((BANDS, PANELS, ROWS, 128), F32),
            vmem((BANDS, 2, ROWS, 128), F32),
            vmem((3 * BANDS, PANELS, ROWS, 128), F32),
            vmem((BANDS, PANELS, ROWS, 128), F32),
            field, field, field, field, field,
            vmem((11, 2, PANELS, CROWS, 128), F32),
            vmem((2, CROWS, 128), F32),
            vmem((2, 16, 128), F32),
            vmem((8, 16, 128), F32),
            vmem((T, 128), F32),
            vmem((2, T // 2, 128), F32),
            vmem((2, T // 2, 128), F32),
            vmem((8, 16, 128), F32),
            vmem((ROWS, 128), F32),
            vmem((ROWS, 128), F32),
            vmem((8, 128), jnp.int32),
            vmem((8, 8, 128), jnp.int32),
            pltpu.SemaphoreType.DMA((4,)),
            pltpu.SemaphoreType.DMA((32,)),
            pltpu.SemaphoreType.DMA((32,)),
        ],
        compiler_params=pltpu.CompilerParams(
            collective_id=0, has_side_effects=True, vmem_limit_bytes=62 * 1024 * 1024
        ),
    )(frame_first, frame_second, shifts)


def solution(mesh):
    return jax.shard_map(
        local,
        mesh=mesh,
        in_specs=(P(None, "row", "col"), P(None, "row", "col"), P("row", "col", None)),
        out_specs=(P(None, "row", "col"), P(None, "row", "col")),
        check_vma=False,
    )
```

time: 57.3 us -> 34.3 us (0.60)
  Pallas kernels: 52 us -> 31 us
  local copies, waits for them, and re-layouts: 4.51 us -> 2.49 us
    pallas_call x1, Pallas kernels: 52 us -> 31 us  [local(): pl.pallas_call(kernel, out_shape=(jax.ShapeDtypeStruct((2, T, T), F32), j...]
    unnamed x8 -> x4, local copies, waits for them, and re-layouts: 4.51 us -> 2.49 us
where the time goes in v2:
time: 34.3 us; the launch traced here: 34.2 us
  Pallas kernels  31 us (90%)
  local copies, waits for them, and re-layouts  2.49 us (7%)
  between operations  0.65 us (2%)
    pallas_call x1, Pallas kernels, local(): pl.pallas_call(kernel, out_shape=(jax.ShapeDtypeStruct((2, T, T), F32), j...  31 us
    unnamed x4, local copies, waits for them, and re-layouts  2.49 us

profile of v2, /device:TPU:1, one launch (start us, length us, event | category | flops | bytes accessed | tf_op | source)
XLA Modules:
  0.0 34.2 jit_solution(9563301062598454798)
XLA Ops:
  0.6 31.0 %shard_map.50 = (f32[2,256,256]{2,1,0:T(8,128)}, f32[2,32,32]{2,1,0:T(8,128)}) custom-call(f32[4,256,256]{2,1,0:T(8,128)} %f1_ref.1, f32[4,256,256]{2,1,0:T(8,128)} %f2_ref.1, s32[1,1,2]{2,1,0:T(1,128)} %sh_ref.1), custom_call_target="tpu_custom_call" | custom-call | tf_op jit(solution)/shard_map/pallas_call | solution.py:499
  31.7 0.0 copy-start
  31.7 1.9 %copy.7 = f32[2,256,256]{2,1,0:T(8,128)} copy(f32[2,256,256]{2,1,0:T(8,128)} %get-tuple-element.4) | data formatting | bytes 1048576
  33.6 0.0 copy-done
  33.6 0.6 %copy.8 = f32[2,32,32]{2,1,0:T(8,128)} copy(f32[2,32,32]{2,1,0:T(8,128)S(1)} %copy-done) | data formatting | bytes 16384
Async XLA Ops:
  31.7 1.9 %copy-start = (f32[2,32,32]{2,1,0:T(8,128)S(1)}, f32[2,32,32]{2,1,0:T(8,128)}, u32[]{:S(2)}) copy-start(f32[2,32,32]{2,1,0:T(8,128)} %get-tuple-element.5) | copy-start | bytes 24580

commit v3 on v2

--- a/solution.py
+++ b/solution.py
@@ -18,6 +18,7 @@
 FIRST = OFF - 8
 STRIPS = T // 8 + 2
 UNROLL = STRIPS // 2
+MOVE = 17
 PANELS = 3
 DEEP = 9
 THIN = 4
@@ -76,7 +77,7 @@
 
 def kernel(
     f1_ref, f2_ref, sh_ref, flow_ref, coarse_ref,
-    s2, f1v, g, a, p1, u, ub, prv, pcv, tc, ce, cs, cr,
+    s2, wv, f1v, g, a, p1, u, ub, prv, pcv, tc, ce, cs, cr,
     pack, es, er, kr, eq, own, shs, shr,
     local_sem, send_sem, recv_sem,
 ):
@@ -131,10 +132,28 @@
         pack[aligned(8 * i), :] = acc
         return carry
 
-    lax.fori_loop(0, T // 8, packing, 0, unroll=8)
+    lax.fori_loop(0, T // 8, packing, 0, unroll=32)
     upper, lower = pack[0:128, :], pack[128:256, :]
     es[0] = jnp.where(tall, upper, roll(lower, 64, 1))
     es[1] = jnp.where(tall, roll(upper, 64, 1), lower)
+
+    pl.semaphore_wait(barrier, len(DIRECTIONS))
+
+    for dr, dc in DIRECTIONS:
+        seen = DIRECTIONS.index((-dr, -dc))
+        if dr != 0 and dc != 0:
+            send(pack.at[pl.ds(0 if dr < 0 else T - 16, 16), :], kr.at[seen], (dr, dc))
+        elif dr == 0:
+            side = 0 if dc < 0 else 1
+            send(es.at[side], er.at[side], (dr, dc))
+        else:
+            from2, to2 = (OFF, OFF + T) if dr < 0 else (OFF + T - DEEP, OFF - DEEP)
+            from1, to1 = (OFF, OFF + T) if dr < 0 else (OFF + T - THIN, OFF - THIN)
+            both = pl.ds(0, 2)
+            send(s2.at[:, both, pl.ds(from2, DEEP), :], s2.at[:, both, pl.ds(to2, DEEP), :], (dr, dc))
+            send(f1v.at[:, both, pl.ds(from1, THIN), :], f1v.at[:, both, pl.ds(to1, THIN), :], (dr, dc))
+        send(shs, shr.at[seen], (dr, dc))
+    raw_count = len(sends)
 
     col_id = lax.broadcasted_iota(jnp.int32, (128, 128), 0) // FACTOR
     lane_id = lax.broadcasted_iota(jnp.int32, (128, 128), 1)
@@ -160,34 +179,16 @@
             piece = ce[frame, 8 + 16 * half:24 + 16 * half, :]
             edge_l = jnp.where(group == n, roll(piece, 8 * n, 1), edge_l)
             edge_r = jnp.where(group == n, roll(piece, 8 * n - 24, 1), edge_r)
-    cs[0] = edge_l
-    cs[1] = edge_r
-
-    pl.semaphore_wait(barrier, len(DIRECTIONS))
-
-    def send_rows(dr, dc, seen):
-        for frame in range(2):
-            send(
-                ce.at[frame, pl.ds(8 if dr < 0 else CT, 8), :], cr.at[seen, pl.ds(8 * frame, 8), :], (dr, dc)
-            )
+    for half in range(2):
+        cs[0, half] = edge_l[8 * half:8 * half + 8]
+        cs[1, half] = edge_r[8 * half:8 * half + 8]
 
     for dr, dc in DIRECTIONS:
         seen = DIRECTIONS.index((-dr, -dc))
-        if dr != 0 and dc != 0:
-            send(pack.at[pl.ds(0 if dr < 0 else T - 16, 16), :], kr.at[seen], (dr, dc))
-            send_rows(dr, dc, seen)
-        elif dr == 0:
-            side = 0 if dc < 0 else 1
-            send(es.at[side], er.at[side], (dr, dc))
-            send(cs.at[side], cr.at[seen], (dr, dc))
+        if dr == 0:
+            send(cs.at[0 if dc < 0 else 1], cr.at[seen], (dr, dc))
         else:
-            send_rows(dr, dc, seen)
-            from2, to2 = (OFF, OFF + T) if dr < 0 else (OFF + T - DEEP, OFF - DEEP)
-            from1, to1 = (OFF, OFF + T) if dr < 0 else (OFF + T - THIN, OFF - THIN)
-            both = pl.ds(0, 2)
-            send(s2.at[:, both, pl.ds(from2, DEEP), :], s2.at[:, both, pl.ds(to2, DEEP), :], (dr, dc))
-            send(f1v.at[:, both, pl.ds(from1, THIN), :], f1v.at[:, both, pl.ds(to1, THIN), :], (dr, dc))
-        send(shs, shr.at[seen], (dr, dc))
+            send(ce.at[:, pl.ds(8 if dr < 0 else CT, 8), :], cr.at[seen], (dr, dc))
 
     def own_edge(start):
         acc = jnp.zeros((8, 128), F32)
@@ -203,7 +204,7 @@
 
     lax.fori_loop(0, T // 8, owning, 0, unroll=8)
 
-    for copy in sends:
+    for copy in sends[:raw_count]:
         copy.wait()
 
     def at(direction):
@@ -244,7 +245,7 @@
         own[rows, :] = jnp.where(theirs, x, own[rows, :])
         return carry
 
-    lax.fori_loop(0, STRIPS + 2, third, 0, unroll=9)
+    lax.fori_loop(0, STRIPS + 2, third, 0, unroll=18)
 
     panel_lane = lax.broadcasted_iota(jnp.int32, (PANELS, 8, 128), 2)
 
@@ -280,8 +281,35 @@
         for c in range(2):
             p1[c, 0:2, rows, :] = pull[c]
 
+    amount = back(my_shift[1])
+    over = panel_lane + my_shift[1] >= 128
+    under = panel_lane + my_shift[1] < 0
+
+    def moving(s, carry):
+        base = FIRST + 8 * s
+        for b in range(BANDS):
+            turned = pltpu.roll(s2[b, :, pl.ds(base + my_shift[0], 8), :], amount, 2)
+            wv[b, :, aligned(base), :] = jnp.where(
+                over, following(turned), jnp.where(under, preceding(turned), turned)
+            )
+        return carry
+
+    lax.fori_loop(0, STRIPS, moving, 0, unroll=MOVE)
+
     def window_loop(i, carry):
-        window(OFF + 8 * i, my_shift)
+        base = OFF + 8 * i
+        rows = aligned(base)
+        pull = [0.0, 0.0]
+        for b in range(BANDS):
+            here = wv[b, :, rows, :]
+            fields = (
+                wv[b, 0:2, pl.ds(base + 1, 8), :] - wv[b, 0:2, pl.ds(base - 1, 8), :],
+                across(here)[:2],
+                SIGMA * (here[:2] - f1v[b, :, rows, :]),
+            )
+            pull = store_data(fields, b, slice(0, 2), rows, pull)
+        for c in range(2):
+            p1[c, 0:2, rows, :] = pull[c]
         return carry
 
     lax.fori_loop(0, T // 8, window_loop, 0, unroll=4)
@@ -323,18 +351,22 @@
     clane = lax.broadcasted_iota(jnp.int32, (CROWS, 128), 1)
     ccol = jnp.where(clane < 64, clane, clane - 128) + me_c * CT
     mask = jnp.where((crow >= 0) & (crow < n_r * CT) & (ccol >= 0) & (ccol < n_c * CT), 1.0, 0.0)
+    for copy in sends[raw_count:]:
+        copy.wait()
     means = []
     for frame in range(2):
         def column(dc):
-            parts = [cr[at((-1, dc)), 8 * frame:8 * frame + 8, :]]
+            parts = [cr[at((-1, dc)), frame]]
             turn = CT * dc
             if dc == 0:
                 parts.append(ce[frame, 8:8 + CT, :])
             else:
                 for half in range(2):
                     n = 2 * frame + half
-                    parts.append(roll(cr[at((0, dc))], (0 if dc > 0 else 24) - 8 * n, 1))
-            parts.append(cr[at((1, dc)), 8 * frame:8 * frame + 8, :])
+                    side = cr[at((0, dc))]
+                    side = jnp.concatenate([side[0], side[1]], axis=0)
+                    parts.append(roll(side, (0 if dc > 0 else 24) - 8 * n, 1))
+            parts.append(cr[at((1, dc)), frame])
             return roll(jnp.concatenate(parts, axis=0), turn, 1)
 
         mine, right, left = column(0), column(1), column(-1)
@@ -510,14 +542,15 @@
         out_specs=(pl.BlockSpec(memory_space=vmem), pl.BlockSpec(memory_space=vmem)),
         scratch_shapes=[
             vmem((BANDS, PANELS, ROWS, 128), F32),
+            vmem((BANDS, PANELS, ROWS, 128), F32),
             vmem((BANDS, 2, ROWS, 128), F32),
             vmem((3 * BANDS, PANELS, ROWS, 128), F32),
             vmem((BANDS, PANELS, ROWS, 128), F32),
             field, field, field, field, field,
             vmem((11, 2, PANELS, CROWS, 128), F32),
             vmem((2, CROWS, 128), F32),
-            vmem((2, 16, 128), F32),
-            vmem((8, 16, 128), F32),
+            vmem((2, 2, 8, 128), F32),
+            vmem((8, 2, 8, 128), F32),
             vmem((T, 128), F32),
             vmem((2, T // 2, 128), F32),
             vmem((2, T // 2, 128), F32),

time: 34.3 us -> 29.6 us (0.86)
  Pallas kernels: 31 us -> 26.3 us
    pallas_call x1, Pallas kernels: 31 us -> 26.3 us  [local(): pl.pallas_call(kernel, out_shape=(jax.ShapeDtypeStruct((2, T, T), F32), j...]
where the time goes in v3:
time: 29.6 us; the launch traced here: 29.5 us
  Pallas kernels  26.3 us (89%)
  local copies, waits for them, and re-layouts  2.49 us (8%)
  between operations  0.65 us (2%)
    pallas_call x1, Pallas kernels, local(): pl.pallas_call(kernel, out_shape=(jax.ShapeDtypeStruct((2, T, T), F32), j...  26.3 us
    unnamed x4, local copies, waits for them, and re-layouts  2.49 us

profile of v3, /device:TPU:1, one launch (start us, length us, event | category | flops | bytes accessed | tf_op | source)
XLA Modules:
  0.0 29.5 jit_solution(16607291224864747015)
XLA Ops:
  0.6 26.3 %shard_map.50 = (f32[2,256,256]{2,1,0:T(8,128)}, f32[2,32,32]{2,1,0:T(8,128)}) custom-call(f32[4,256,256]{2,1,0:T(8,128)} %f1_ref.1, f32[4,256,256]{2,1,0:T(8,128)} %f2_ref.1, s32[1,1,2]{2,1,0:T(1,128)} %sh_ref.1), custom_call_target="tpu_custom_call" | custom-call | tf_op jit(solution)/shard_map/pallas_call | solution.py:531
  27.0 0.0 copy-start
  27.0 1.9 %copy.7 = f32[2,256,256]{2,1,0:T(8,128)} copy(f32[2,256,256]{2,1,0:T(8,128)} %get-tuple-element.4) | data formatting | bytes 1048576
  28.9 0.0 copy-done
  28.9 0.6 %copy.8 = f32[2,32,32]{2,1,0:T(8,128)} copy(f32[2,32,32]{2,1,0:T(8,128)S(1)} %copy-done) | data formatting | bytes 16384
Async XLA Ops:
  27.0 1.9 %copy-start = (f32[2,32,32]{2,1,0:T(8,128)S(1)}, f32[2,32,32]{2,1,0:T(8,128)}, u32[]{:S(2)}) copy-start(f32[2,32,32]{2,1,0:T(8,128)} %get-tuple-element.5) | copy-start | bytes 24580

commit v4 on v3

--- a/solution.py
+++ b/solution.py
@@ -18,7 +18,8 @@
 FIRST = OFF - 8
 STRIPS = T // 8 + 2
 UNROLL = STRIPS // 2
-MOVE = 17
+MOVE = 16
+EDGE = 10
 PANELS = 3
 DEEP = 9
 THIN = 4
@@ -112,7 +113,7 @@
             device_id=device(direction), device_id_type=pl.DeviceIdType.MESH,
         )
         copy.start()
-        sends.append(copy)
+        sends.append((copy, direction[0] != 0 and direction[1] != 0))
 
     lane = lax.broadcasted_iota(jnp.int32, (8, 128), 1)
     place = lane % 16
@@ -204,32 +205,29 @@
 
     lax.fori_loop(0, T // 8, owning, 0, unroll=8)
 
-    for copy in sends[:raw_count]:
-        copy.wait()
+    for copy, diagonal in sends[:raw_count]:
+        if not diagonal:
+            copy.wait()
 
     def at(direction):
         return DIRECTIONS.index(direction)
 
-    shift_at = {d: (shr[at(d), 0, 0], shr[at(d), 1, 0]) for d in DIRECTIONS}
+    def shift_at(d):
+        return shr[at(d), 0, 0], shr[at(d), 1, 0]
 
     keep_lane = jnp.where(
         lane[0:1] < 64, jnp.where(me_c == n_c - 1, 0.0, 1.0), jnp.where(me_c == 0, 0.0, 1.0)
     )
     eq[OFF:OFF + 128, :] = jnp.where(tall, er[0], roll(er[1], 64, 1)) * keep_lane
     eq[OFF + 128:OFF + 256, :] = jnp.where(tall, roll(er[0], 64, 1), er[1]) * keep_lane
-    side16 = lax.broadcasted_iota(jnp.int32, (16, 128), 1) < 64
-    eq[OFF - 16:OFF, :] = jnp.where(side16, kr[at((-1, 1))], kr[at((-1, -1))]) * keep_lane
-    eq[OFF + T:OFF + T + 16, :] = jnp.where(side16, kr[at((1, 1))], kr[at((1, -1))]) * keep_lane
 
     @pl.when(me_r == 0)
     def _():
         s2[:, 0:2, OFF - 16:OFF, :] = jnp.zeros((BANDS, 2, 16, 128), F32)
-        eq[OFF - 16:OFF, :] = jnp.zeros((16, 128), F32)
 
     @pl.when(me_r == n_r - 1)
     def _():
         s2[:, 0:2, OFF + T:OFF + T + 16, :] = jnp.zeros((BANDS, 2, 16, 128), F32)
-        eq[OFF + T:OFF + T + 16, :] = jnp.zeros((16, 128), F32)
 
     for start in (OFF - 16, OFF - 8, OFF + T, OFF + T + 8):
         own[start:start + 8, :] = own_edge(start)
@@ -245,7 +243,7 @@
         own[rows, :] = jnp.where(theirs, x, own[rows, :])
         return carry
 
-    lax.fori_loop(0, STRIPS + 2, third, 0, unroll=18)
+    lax.fori_loop(2, STRIPS, third, 0, unroll=16)
 
     panel_lane = lax.broadcasted_iota(jnp.int32, (PANELS, 8, 128), 2)
 
@@ -294,7 +292,7 @@
             )
         return carry
 
-    lax.fori_loop(0, STRIPS, moving, 0, unroll=MOVE)
+    lax.fori_loop(1, STRIPS - 1, moving, 0, unroll=MOVE)
 
     def window_loop(i, carry):
         base = OFF + 8 * i
@@ -312,9 +310,7 @@
             p1[c, 0:2, rows, :] = pull[c]
         return carry
 
-    lax.fori_loop(0, T // 8, window_loop, 0, unroll=4)
-    window(OFF - 8, shift_at[(-1, 0)])
-    window(OFF + T, shift_at[(1, 0)])
+    lax.fori_loop(1, T // 8 - 1, window_loop, 0, unroll=5)
 
     def edge(base, right, left):
         rows = aligned(base)
@@ -339,19 +335,43 @@
         for c in range(2):
             p1[c, 2, rows, :] = pull[c]
 
+    side_shifts = shift_at((0, 1)), shift_at((0, -1))
+
     def edge_loop(i, carry):
-        edge(OFF + 8 * i, shift_at[(0, 1)], shift_at[(0, -1)])
-        return carry
-
-    lax.fori_loop(0, T // 8, edge_loop, 0, unroll=8)
-    edge(OFF - 8, shift_at[(-1, 1)], shift_at[(-1, -1)])
-    edge(OFF + T, shift_at[(1, 1)], shift_at[(1, -1)])
+        edge(OFF + 8 * i, *side_shifts)
+        return carry
+
+    lax.fori_loop(1, T // 8 - 1, edge_loop, 0, unroll=EDGE)
+
+    for copy, diagonal in sends[:raw_count]:
+        if diagonal:
+            copy.wait()
+    keep_above = jnp.where(me_r == 0, 0.0, 1.0) * keep_lane
+    keep_below = jnp.where(me_r == n_r - 1, 0.0, 1.0) * keep_lane
+    side16 = lax.broadcasted_iota(jnp.int32, (16, 128), 1) < 64
+    eq[OFF - 16:OFF, :] = jnp.where(side16, kr[at((-1, 1))], kr[at((-1, -1))]) * keep_above
+    eq[OFF + T:OFF + T + 16, :] = jnp.where(side16, kr[at((1, 1))], kr[at((1, -1))]) * keep_below
+    for i in (0, 1, STRIPS, STRIPS + 1):
+        third(i, 0)
+
+    def outermost(j, carry):
+        moving(j * (STRIPS - 1), 0)
+        moving(j * (STRIPS - 3) + 1, 0)
+        return carry
+
+    lax.fori_loop(0, 2, outermost, 0, unroll=2)
+    lax.fori_loop(0, 2, lambda j, carry: window_loop(j * (T // 8 - 1), carry), 0, unroll=2)
+    window(OFF - 8, shift_at((-1, 0)))
+    window(OFF + T, shift_at((1, 0)))
+    lax.fori_loop(0, 2, lambda j, carry: edge_loop(j * (T // 8 - 1), carry), 0, unroll=2)
+    edge(OFF - 8, shift_at((-1, 1)), shift_at((-1, -1)))
+    edge(OFF + T, shift_at((1, 1)), shift_at((1, -1)))
 
     crow = lax.broadcasted_iota(jnp.int32, (CROWS, 128), 0) - 8 + me_r * CT
     clane = lax.broadcasted_iota(jnp.int32, (CROWS, 128), 1)
     ccol = jnp.where(clane < 64, clane, clane - 128) + me_c * CT
     mask = jnp.where((crow >= 0) & (crow < n_r * CT) & (ccol >= 0) & (ccol < n_c * CT), 1.0, 0.0)
-    for copy in sends[raw_count:]:
+    for copy, _ in sends[raw_count:]:
         copy.wait()
     means = []
     for frame in range(2):
@@ -531,8 +551,8 @@
     return pl.pallas_call(
         kernel,
         out_shape=(
-            jax.ShapeDtypeStruct((2, T, T), F32),
-            jax.ShapeDtypeStruct((2, CT, CT), F32),
+            vmem((2, T, T), F32),
+            vmem((2, CT, CT), F32),
         ),
         in_specs=[
             pl.BlockSpec(memory_space=pl.ANY),
@@ -564,7 +584,7 @@
             pltpu.SemaphoreType.DMA((32,)),
         ],
         compiler_params=pltpu.CompilerParams(
-            collective_id=0, has_side_effects=True, vmem_limit_bytes=62 * 1024 * 1024
+            collective_id=0, has_side_effects=True, vmem_limit_bytes=60 * 1024 * 1024
         ),
     )(frame_first, frame_second, shifts)
 

time: 29.6 us -> 27.3 us (0.922)
  the two profiles are of different devices: /device:TPU:1 before, /device:TPU:6 now
where the time goes in v4:
time: 27.3 us; the launch traced here: 27.2 us
  Pallas kernels  25.2 us (92%)
  local copies, waits for them, and re-layouts  1.41 us (5%)
  between operations  0.64 us (2%)
    pallas_call x1, Pallas kernels, local(): pl.pallas_call(kernel, out_shape=(vmem((2, T, T), F32), vmem((2, CT, CT),...  25.2 us
    unnamed x2, local copies, waits for them, and re-layouts  1.41 us

profile of v4, /device:TPU:6, one launch (start us, length us, event | category | flops | bytes accessed | tf_op | source)
XLA Modules:
  0.0 27.2 jit_solution(13325821859974266794)
XLA Ops:
  0.6 25.2 %shard_map.50 = (f32[2,256,256]{2,1,0:T(8,128)S(1)}, f32[2,32,32]{2,1,0:T(8,128)S(1)}) custom-call(f32[4,256,256]{2,1,0:T(8,128)} %f1_ref.1, f32[4,256,256]{2,1,0:T(8,128)} %f2_ref.1, s32[1,1,2]{2,1,0:T(1,128)} %sh_ref.1), custom_call_target="tpu_custom_call" | custom-call | tf_op jit(solution)/shard_map/pallas_call | solution.py:551
  25.8 0.8 %copy.7 = f32[2,256,256]{2,1,0:T(8,128)} copy(f32[2,256,256]{2,1,0:T(8,128)S(1)} %get-tuple-element.2) | data formatting | bytes 1048576
  26.6 0.6 %copy.8 = f32[2,32,32]{2,1,0:T(8,128)} copy(f32[2,32,32]{2,1,0:T(8,128)S(1)} %get-tuple-element.3) | data formatting | bytes 16384

commit v5 on v4

--- a/solution.py
+++ b/solution.py
@@ -89,9 +89,16 @@
         dr, dc = direction
         return (lax.rem(me_r + dr + n_r, n_r), lax.rem(me_c + dc + n_c, n_c))
 
+    def exists(direction):
+        row, col = me_r + direction[0], me_c + direction[1]
+        return (row >= 0) & (row < n_r) & (col >= 0) & (col < n_c)
+
+    present = {d: exists(d) for d in DIRECTIONS}
     barrier = pltpu.get_barrier_semaphore()
     for direction in DIRECTIONS:
-        pl.semaphore_signal(barrier, inc=1, device_id=device(direction), device_id_type=pl.DeviceIdType.MESH)
+        @pl.when(present[direction])
+        def _():
+            pl.semaphore_signal(barrier, inc=1, device_id=device(direction), device_id_type=pl.DeviceIdType.MESH)
     gets = []
     for ref, kept in ((f2_ref, s2), (f1_ref, f1v)):
         for k in range(2):
@@ -104,6 +111,19 @@
     sub8 = lax.broadcasted_iota(jnp.int32, (8, 128), 0)
     shs[...] = jnp.where(sub8 == 0, my_shift[0], my_shift[1])
 
+    for direction in DIRECTIONS:
+        @pl.when(jnp.logical_not(present[direction]))
+        def _():
+            n = DIRECTIONS.index(direction)
+            shr[n] = jnp.zeros((8, 128), jnp.int32)
+            cr[n] = jnp.zeros((2, 8, 128), F32)
+            kr[n] = jnp.zeros((16, 128), F32)
+            if direction[0] == 0:
+                er[0 if direction[1] > 0 else 1] = jnp.zeros((T // 2, 128), F32)
+            if direction[1] == 0:
+                base = OFF - 8 if direction[0] < 0 else OFF + T
+                f1v[:, :, base:base + 8, :] = jnp.zeros((BANDS, 2, 8, 128), F32)
+
     sends = []
 
     def send(src, dst, direction):
@@ -112,8 +132,29 @@
             src_ref=src, dst_ref=dst, send_sem=send_sem.at[slot], recv_sem=recv_sem.at[slot],
             device_id=device(direction), device_id_type=pl.DeviceIdType.MESH,
         )
-        copy.start()
-        sends.append((copy, direction[0] != 0 and direction[1] != 0))
+        sends.append((copy, direction))
+
+    def start(copies):
+        for direction in DIRECTIONS:
+            @pl.when(present[direction])
+            def _():
+                for copy, way in copies:
+                    if way == direction:
+                        copy.start()
+
+    def finish(copies):
+        for direction in DIRECTIONS:
+            ours = [copy for copy, way in copies if way == direction]
+            if ours:
+                @pl.when(present[direction])
+                def _():
+                    for copy in ours:
+                        copy.wait_send()
+
+                @pl.when(present[-direction[0], -direction[1]])
+                def _():
+                    for copy in ours:
+                        copy.wait_recv()
 
     lane = lax.broadcasted_iota(jnp.int32, (8, 128), 1)
     place = lane % 16
@@ -138,7 +179,7 @@
     es[0] = jnp.where(tall, upper, roll(lower, 64, 1))
     es[1] = jnp.where(tall, roll(upper, 64, 1), lower)
 
-    pl.semaphore_wait(barrier, len(DIRECTIONS))
+    pl.semaphore_wait(barrier, sum(here.astype(jnp.int32) for here in present.values()))
 
     for dr, dc in DIRECTIONS:
         seen = DIRECTIONS.index((-dr, -dc))
@@ -154,7 +195,8 @@
             send(s2.at[:, both, pl.ds(from2, DEEP), :], s2.at[:, both, pl.ds(to2, DEEP), :], (dr, dc))
             send(f1v.at[:, both, pl.ds(from1, THIN), :], f1v.at[:, both, pl.ds(to1, THIN), :], (dr, dc))
         send(shs, shr.at[seen], (dr, dc))
-    raw_count = len(sends)
+    raw_sends = list(sends)
+    start(raw_sends)
 
     col_id = lax.broadcasted_iota(jnp.int32, (128, 128), 0) // FACTOR
     lane_id = lax.broadcasted_iota(jnp.int32, (128, 128), 1)
@@ -190,6 +232,8 @@
             send(cs.at[0 if dc < 0 else 1], cr.at[seen], (dr, dc))
         else:
             send(ce.at[:, pl.ds(8 if dr < 0 else CT, 8), :], cr.at[seen], (dr, dc))
+    coarse_sends = sends[len(raw_sends):]
+    start(coarse_sends)
 
     def own_edge(start):
         acc = jnp.zeros((8, 128), F32)
@@ -205,9 +249,7 @@
 
     lax.fori_loop(0, T // 8, owning, 0, unroll=8)
 
-    for copy, diagonal in sends[:raw_count]:
-        if not diagonal:
-            copy.wait()
+    finish([(copy, way) for copy, way in raw_sends if 0 in way])
 
     def at(direction):
         return DIRECTIONS.index(direction)
@@ -343,9 +385,7 @@
 
     lax.fori_loop(1, T // 8 - 1, edge_loop, 0, unroll=EDGE)
 
-    for copy, diagonal in sends[:raw_count]:
-        if diagonal:
-            copy.wait()
+    finish([(copy, way) for copy, way in raw_sends if 0 not in way])
     keep_above = jnp.where(me_r == 0, 0.0, 1.0) * keep_lane
     keep_below = jnp.where(me_r == n_r - 1, 0.0, 1.0) * keep_lane
     side16 = lax.broadcasted_iota(jnp.int32, (16, 128), 1) < 64
@@ -371,8 +411,7 @@
     clane = lax.broadcasted_iota(jnp.int32, (CROWS, 128), 1)
     ccol = jnp.where(clane < 64, clane, clane - 128) + me_c * CT
     mask = jnp.where((crow >= 0) & (crow < n_r * CT) & (ccol >= 0) & (ccol < n_c * CT), 1.0, 0.0)
-    for copy, _ in sends[raw_count:]:
-        copy.wait()
+    finish(coarse_sends)
     means = []
     for frame in range(2):
         def column(dc):

time: 27.3 us -> 24.9 us (0.912)
  the two profiles are of different devices: /device:TPU:6 before, /device:TPU:24 now
where the time goes in v5:
time: 24.9 us; the launch traced here: 24.8 us
  Pallas kernels  22.8 us (92%)
  local copies, waits for them, and re-layouts  1.41 us (6%)
  between operations  0.64 us (3%)
    pallas_call x1, Pallas kernels, local(): pl.pallas_call(kernel, out_shape=(vmem((2, T, T), F32), vmem((2, CT, CT),...  22.8 us
    unnamed x2, local copies, waits for them, and re-layouts  1.41 us

profile of v5, /device:TPU:24, one launch (start us, length us, event | category | flops | bytes accessed | tf_op | source)
XLA Modules:
  0.0 24.8 jit_solution(14361968103836026120)
XLA Ops:
  0.6 22.8 %shard_map.50 = (f32[2,256,256]{2,1,0:T(8,128)S(1)}, f32[2,32,32]{2,1,0:T(8,128)S(1)}) custom-call(f32[4,256,256]{2,1,0:T(8,128)} %f1_ref.1, f32[4,256,256]{2,1,0:T(8,128)} %f2_ref.1, s32[1,1,2]{2,1,0:T(1,128)} %sh_ref.1), custom_call_target="tpu_custom_call" | custom-call | tf_op jit(solution)/shard_map/pallas_call | solution.py:590
  23.4 0.8 %copy.7 = f32[2,256,256]{2,1,0:T(8,128)} copy(f32[2,256,256]{2,1,0:T(8,128)S(1)} %get-tuple-element.2) | data formatting | bytes 1048576
  24.2 0.6 %copy.8 = f32[2,32,32]{2,1,0:T(8,128)} copy(f32[2,32,32]{2,1,0:T(8,128)S(1)} %get-tuple-element.3) | data formatting | bytes 16384

commit v6 on v5

--- a/solution.py
+++ b/solution.py
@@ -17,7 +17,7 @@
 ROWS = T + 2 * OFF
 FIRST = OFF - 8
 STRIPS = T // 8 + 2
-UNROLL = STRIPS // 2
+UNROLL = STRIPS
 MOVE = 16
 EDGE = 10
 PANELS = 3
@@ -26,7 +26,7 @@
 CROWS = CT + 16
 F32 = jnp.float32
 BF16 = jnp.bfloat16
-DIRECTIONS = [(-1, -1), (-1, 1), (1, -1), (1, 1), (0, -1), (0, 1), (-1, 0), (1, 0)]
+DIRECTIONS = [(0, -1), (0, 1), (-1, -1), (-1, 1), (1, -1), (1, 1), (-1, 0), (1, 0)]
 
 
 def split3(x):
@@ -352,7 +352,7 @@
             p1[c, 0:2, rows, :] = pull[c]
         return carry
 
-    lax.fori_loop(1, T // 8 - 1, window_loop, 0, unroll=5)
+    lax.fori_loop(1, T // 8 - 1, window_loop, 0, unroll=10)
 
     def edge(base, right, left):
         rows = aligned(base)
@@ -581,7 +581,7 @@
             lax.fori_loop(0, STRIPS, primal, 0, unroll=UNROLL)
             clear_rows(ub)
         else:
-            lax.fori_loop(1, STRIPS - 1, primal, 0, unroll=8)
+            lax.fori_loop(1, STRIPS - 1, primal, 0, unroll=16)
 
 
 def local(frame_first, frame_second, shifts):

time: 24.9 us -> 23.9 us (0.960)
  Pallas kernels: 22.8 us -> 21.7 us
    pallas_call x1, Pallas kernels: 22.8 us -> 21.7 us  [local(): pl.pallas_call(kernel, out_shape=(vmem((2, T, T), F32), vmem((2, CT, CT),...]
where the time goes in v6:
time: 23.9 us; the launch traced here: 23.8 us
  Pallas kernels  21.7 us (91%)
  local copies, waits for them, and re-layouts  1.41 us (6%)
  between operations  0.64 us (3%)
    pallas_call x1, Pallas kernels, local(): pl.pallas_call(kernel, out_shape=(vmem((2, T, T), F32), vmem((2, CT, CT),...  21.7 us
    unnamed x2, local copies, waits for them, and re-layouts  1.41 us

profile of v6, /device:TPU:24, one launch (start us, length us, event | category | flops | bytes accessed | tf_op | source)
XLA Modules:
  0.0 23.8 jit_solution(16758739298496508524)
XLA Ops:
  0.6 21.7 %shard_map.50 = (f32[2,256,256]{2,1,0:T(8,128)S(1)}, f32[2,32,32]{2,1,0:T(8,128)S(1)}) custom-call(f32[4,256,256]{2,1,0:T(8,128)} %f1_ref.1, f32[4,256,256]{2,1,0:T(8,128)} %f2_ref.1, s32[1,1,2]{2,1,0:T(1,128)} %sh_ref.1), custom_call_target="tpu_custom_call" | custom-call | tf_op jit(solution)/shard_map/pallas_call | solution.py:590
  22.4 0.8 %copy.7 = f32[2,256,256]{2,1,0:T(8,128)} copy(f32[2,256,256]{2,1,0:T(8,128)S(1)} %get-tuple-element.2) | data formatting | bytes 1048576
  23.2 0.6 %copy.8 = f32[2,32,32]{2,1,0:T(8,128)} copy(f32[2,32,32]{2,1,0:T(8,128)S(1)} %get-tuple-element.3) | data formatting | bytes 16384

commit v7 on v6

--- a/solution.py
+++ b/solution.py
@@ -352,7 +352,7 @@
             p1[c, 0:2, rows, :] = pull[c]
         return carry
 
-    lax.fori_loop(1, T // 8 - 1, window_loop, 0, unroll=10)
+    lax.fori_loop(1, T // 8 - 1, window_loop, 0, unroll=15)
 
     def edge(base, right, left):
         rows = aligned(base)
@@ -581,7 +581,7 @@
             lax.fori_loop(0, STRIPS, primal, 0, unroll=UNROLL)
             clear_rows(ub)
         else:
-            lax.fori_loop(1, STRIPS - 1, primal, 0, unroll=16)
+            lax.fori_loop(1, STRIPS - 1, primal, 0, unroll=32)
 
 
 def local(frame_first, frame_second, shifts):

time: 23.9 us -> 23.7 us (level)
  no operation moved by 1% of the time
where the time goes in v7:
time: 23.7 us; the launch traced here: 23.6 us
  Pallas kernels  21.6 us (91%)
  local copies, waits for them, and re-layouts  1.41 us (6%)
  between operations  0.64 us (3%)
    pallas_call x1, Pallas kernels, local(): pl.pallas_call(kernel, out_shape=(vmem((2, T, T), F32), vmem((2, CT, CT),...  21.6 us
    unnamed x2, local copies, waits for them, and re-layouts  1.41 us

profile of v7, /device:TPU:24, one launch (start us, length us, event | category | flops | bytes accessed | tf_op | source)
XLA Modules:
  0.0 23.6 jit_solution(11400773048146365911)
XLA Ops:
  0.6 21.6 %shard_map.50 = (f32[2,256,256]{2,1,0:T(8,128)S(1)}, f32[2,32,32]{2,1,0:T(8,128)S(1)}) custom-call(f32[4,256,256]{2,1,0:T(8,128)} %f1_ref.1, f32[4,256,256]{2,1,0:T(8,128)} %f2_ref.1, s32[1,1,2]{2,1,0:T(1,128)} %sh_ref.1), custom_call_target="tpu_custom_call" | custom-call | tf_op jit(solution)/shard_map/pallas_call | solution.py:590
  22.2 0.8 %copy.7 = f32[2,256,256]{2,1,0:T(8,128)} copy(f32[2,256,256]{2,1,0:T(8,128)S(1)} %get-tuple-element.2) | data formatting | bytes 1048576
  23.0 0.6 %copy.8 = f32[2,32,32]{2,1,0:T(8,128)} copy(f32[2,32,32]{2,1,0:T(8,128)S(1)} %get-tuple-element.3) | data formatting | bytes 16384
